TPU v7x, 32 devices: a whole 2x2x4 slice. The times are simulated.
32 devices in a mesh: head: 2 (over x), clus: 16 (over z, y, core).
Axes of the slice: x: 2, y: 2, z: 4, core: 2. Of those that a mesh axis runs over, the one named last changes fastest.
Arguments:
- key_cache: bfloat16 [2, 16384, 1024], P('head', 'clus'), may hold values from -8 to 8
- value_cache: bfloat16 [2, 16384, 1024], P('head', 'clus'), may hold values from -6 to 6
- prompt_queries: bfloat16 [64, 8192], P(None, 'head'), may hold values from -64 to 64
- tile_cluster: int32 [8, 16, 2, 8, 1], P('head', 'clus'), may hold values from 0 to 15; in each aligned block of 16 rows (0 to 15, 16 to 31, ..., all dimensions but the last counted through in order) no two rows name the same one
- listed_clusters: int32 [8, 4, 4], P('head'), may hold values from 0 to 15, as said below
Outputs:
- attended: bfloat16 [64, 8192], P('clus', 'head')
Inputs may be any that keep to these rules, and one draw needn't show every extreme that they name: `tile_cluster`: among the 16 tiles of one index of clus and one KV head (the aligned blocks of rows in the order head, clus, slab, tile), no cluster is named more than 1 times, and some block names one cluster exactly 1 times. `listed_clusters`: each row names 4 distinct clusters.
All inputs are finite; a program needn't handle non-finite values.
Results may differ from a plain program's by a relative error of at most 0.0085.
Values may be sent and summed in bfloat16 or wider, within the bound.
A program may use at most 64 MiB of HBM per device.

v0:
```python
import jax
import jax.numpy as jnp
from jax import lax
from jax.sharding import PartitionSpec as P

DH = 128
GROUP = 8
TILE = 128
QBLK = 16


floor_value = -1e30
highest = lax.Precision.HIGHEST


def combined_all(shard, axis, combine):
    everything = jax.tree.map(lambda part: lax.all_gather(part, axis), shard)
    leading = jax.tree.map(lambda part: part[0], everything)

    def turn(k, so_far):
        return combine(so_far, jax.tree.map(lambda part: part[k], everything))

    return lax.fori_loop(1, lax.axis_size(axis), turn, leading)


def block_partials(
    query_blocks, key_rows, value_rows, tile_mask, key_mean, value_sum, counts_mine, approx_on
):
    score_scale = key_rows.shape[-1] ** (-0.5)
    tile_rows = key_rows.shape[0] // tile_mask.shape[-1]

    def one_block(block_inputs):
        block_queries, mask_tiles, approx_flag = block_inputs
        key_mask = jnp.repeat(mask_tiles, tile_rows) > 0.5
        scores = (
            jnp.einsum("rd,kd->rk", block_queries, key_rows, preferred_element_type=jnp.float32)
            * score_scale
        )
        approx_score = (
            jnp.dot(block_queries.astype(jnp.float32), key_mean, precision=highest) * score_scale
        )
        approx_live = approx_flag > 0.5
        row_top = jnp.maximum(
            jnp.max(jnp.where(key_mask[None, :], scores, floor_value), axis=1),
            jnp.where(approx_live, approx_score, floor_value),
        )
        weights = jnp.where(key_mask[None, :], jnp.exp(scores - row_top[:, None]), 0.0)
        probabilities = weights.astype(jnp.bfloat16)
        approx_weight = jnp.where(approx_live, jnp.exp(approx_score - row_top), 0.0)
        row_total = jnp.sum(weights, axis=1) + counts_mine * approx_weight
        numerator = jnp.dot(probabilities, value_rows, preferred_element_type=jnp.float32)
        numerator = numerator + approx_weight[:, None] * value_sum[None, :]
        return (row_top, row_total, numerator)

    return lax.map(one_block, (query_blocks, tile_mask, approx_on))


def combine_parts(first_part, second_part):
    top_first, total_first, numer_first = first_part
    top_second, total_second, numer_second = second_part
    joined = jnp.maximum(top_first, top_second)
    factor_first = jnp.exp(top_first - joined)
    factor_second = jnp.exp(top_second - joined)
    return (
        joined,
        total_first * factor_first + total_second * factor_second,
        numer_first * factor_first[..., None] + numer_second * factor_second[..., None],
    )


def local(key_cache, value_cache, prompt_queries, tile_cluster, listed_clusters):
    owners = lax.axis_size("clus")
    owner_index = lax.axis_index("clus")
    moved_keys, moved_values = (
        lax.all_to_all(key_cache, "head", split_axis=2, concat_axis=0, tiled=True),
        lax.all_to_all(value_cache, "head", split_axis=2, concat_axis=0, tiled=True),
    )
    slab_count, slab_rows, feature_width = moved_keys.shape
    heads_dev = feature_width // DH
    tiles_dev = slab_count * slab_rows // TILE

    def to_tiles(moved):
        shaped = moved.reshape(slab_count, slab_rows // TILE, TILE, heads_dev, DH)
        return shaped.transpose(3, 0, 1, 2, 4).reshape(heads_dev, tiles_dev, TILE, DH)

    key_tiles = to_tiles(moved_keys)
    value_tiles = to_tiles(moved_values)
    cluster_ids = tile_cluster.reshape(heads_dev, tiles_dev)
    column_ids = jnp.arange(owners, dtype=jnp.int32)
    member = (cluster_ids[:, :, None] == column_ids[None, None, :]).astype(jnp.float32)
    listed_mask = jnp.max(
        (listed_clusters[:, :, :, None] == column_ids).astype(jnp.float32), axis=2
    )
    owner_hot = (column_ids == owner_index).astype(jnp.float32)
    mine_listed = jnp.einsum("hbc,c->hb", listed_mask, owner_hot, precision=highest)
    query_count = prompt_queries.shape[0]
    block_count = query_count // QBLK
    query_blocks = prompt_queries.reshape(query_count, heads_dev, GROUP, DH).transpose(1, 0, 2, 3)
    query_blocks = query_blocks.reshape(heads_dev, block_count, QBLK * GROUP, DH)
    key_rows = key_tiles.reshape(heads_dev, tiles_dev * TILE, DH)
    value_rows = value_tiles.reshape(heads_dev, tiles_dev * TILE, DH)
    unit_rows = jnp.ones((TILE,), jnp.bfloat16)
    tile_keys = jnp.einsum("htrd,r->htd", key_tiles, unit_rows, preferred_element_type=jnp.float32)
    tile_values = jnp.einsum(
        "htrd,r->htd", value_tiles, unit_rows, preferred_element_type=jnp.float32
    )
    local_keys = jnp.einsum("htc,htd->hcd", member, tile_keys, precision=highest)
    local_values = jnp.einsum("htc,htd->hcd", member, tile_values, precision=highest)
    local_counts = TILE * jnp.sum(member, axis=1)
    total_keys, total_values, total_counts = lax.psum(
        (local_keys, local_values, local_counts), "clus"
    )
    key_sum = jnp.einsum("hcd,c->hd", total_keys, owner_hot, precision=highest)
    value_sum = jnp.einsum("hcd,c->hd", total_values, owner_hot, precision=highest)
    counts_mine = jnp.einsum("hc,c->h", total_counts, owner_hot, precision=highest)
    tile_mask = jnp.einsum("hbc,htc->hbt", listed_mask, member, precision=highest)
    key_mean = key_sum / jnp.maximum(counts_mine, 1.0)[:, None]
    approx_on = (1.0 - mine_listed) * (counts_mine > 0.5).astype(jnp.float32)[:, None]
    row_top, row_total, numerator = jax.vmap(block_partials)(
        query_blocks, key_rows, value_rows, tile_mask, key_mean, value_sum, counts_mine, approx_on
    )
    row_top = row_top.reshape(heads_dev, query_count, GROUP)
    row_total = row_total.reshape(heads_dev, query_count, GROUP)
    numerator = numerator.reshape(heads_dev, query_count, GROUP, DH)
    share_rows = query_count // owners
    merged_top, merged_total, merged_numer = combined_all(
        (row_top, row_total, numerator), "clus", combine_parts
    )
    kept_total = lax.dynamic_slice_in_dim(merged_total, owner_index * share_rows, share_rows, 1)
    kept_numer = lax.dynamic_slice_in_dim(merged_numer, owner_index * share_rows, share_rows, 1)
    attended = kept_numer / kept_total[..., None]
    return (
        attended.transpose(1, 0, 2, 3)
        .reshape(share_rows, heads_dev * GROUP * DH)
        .astype(jnp.bfloat16)
    )


def solution(mesh):
    placed = (
        P("head", "clus", None),
        P("head", "clus", None),
        P(None, "head"),
        P("head", "clus", None, None, None),
        P("head", None, None),
    )
    return jax.shard_map(
        local, mesh=mesh, in_specs=placed, out_specs=P("clus", "head"), check_vma=False
    )
```

profile of v0, /device:TPU:0, one launch (start us, length us, event | category | flops | bytes accessed | tf_op | source)
XLA Modules:
  0.0 394.4 jit_solution(18138740183464618232)
XLA Ops:
  6.5 10.8 %copy.90 = bf16[1,1024,1024]{1,0,2:T(2,128)(2,1)} copy(bf16[1,1024,1024]{2,1,0:T(8,128)(2,1)} %param.9) | data formatting | bytes 4194304 | tf_op args[0]
  17.4 0.5 broadcast.88
  17.9 12.8 %reduce.4 = bf16[1024,1024]{1,0:T(8,128)(2,1)S(1)} reduce(bf16[1024,1,1024]{2,1,0:T(2,128)(2,1)} %bitcast.195, bf16[]{:T(256)} %broadcast.88), dimensions={1}, to_apply=%bitcast.132.reduce_sub_computation | reduce | bytes 4194306
  30.7 2.5 reshape.74
  33.2 4.2 %all-to-all-start = ((bf16[2,2,262144]{2,1,0:T(2,128)(2,1)}), bf16[2,2,262144]{2,1,0:T(2,128)(2,1)S(1)}, u32[]{:S(2)}, u32[]{:S(2)}) async-start(bf16[2,2,262144]{2,1,0:T(2,128)(2,1)} %reshape.74), calls=%async_computation | async-start | bytes 4194304 | tf_op jit(solution)/shard_map/all_to_all | solution.py:75
  37.4 0.5 broadcast.85
  37.9 0.7 reduce.3
  38.6 10.8 %copy.93 = bf16[1,1024,1024]{1,0,2:T(2,128)(2,1)} copy(bf16[1,1024,1024]{2,1,0:T(8,128)(2,1)} %param.10) | data formatting | bytes 4194304 | tf_op args[1]
  49.5 14.2 %reduce.5 = bf16[1024,1024]{1,0:T(8,128)(2,1)} reduce(bf16[1024,1,1024]{2,1,0:T(2,128)(2,1)} %bitcast.196, bf16[]{:T(256)} %broadcast.88), dimensions={1}, to_apply=%bitcast.134.reduce_sub_computation | reduce | bytes 4194306
  63.6 3.8 reshape.76
  67.5 4.8 %all-to-all-start.1 = ((bf16[2,2,262144]{2,1,0:T(2,128)(2,1)}), bf16[2,2,262144]{2,1,0:T(2,128)(2,1)}, u32[]{:S(2)}, u32[]{:S(2)}) async-start(bf16[2,2,262144]{2,1,0:T(2,128)(2,1)} %reshape.76), calls=%async_computation.1 | async-start | bytes 4194304 | tf_op jit(solution)/shard_map/all_to_all | solution.py:76
  72.7 0.6 broadcast_multiply_fusion
  73.4 3.1 reshape.75
  76.5 3.0 copy.131
  79.5 2.0 copy.121
  81.5 3.2 copy.91
  84.7 0.4 fusion.47
  85.1 0.8 fusion.31
  85.8 12.5 %all-to-all-done.1 = bf16[2,2,262144]{2,1,0:T(2,128)(2,1)} async-done(((bf16[2,2,262144]{2,1,0:T(2,128)(2,1)}), bf16[2,2,262144]{2,1,0:T(2,128)(2,1)}, u32[]{:S(2)}, u32[]{:S(2)}) %all-to-all-start.1) | async-done | bytes 2097184 | tf_op jit(solution)/shard_map/all_to_all | solution.py:76
  98.3 4.3 %reshape.77 = bf16[1024,1,1024]{2,1,0:T(2,128)(2,1)} reshape(bf16[2,2,262144]{2,1,0:T(2,128)(2,1)} %all-to-all-done.1) | data formatting | bytes 4194304
  102.6 3.0 copy.130
  105.6 1.9 copy.122
  107.5 4.3 %copy.94 = bf16[4,2,8,128,128]{4,3,2,1,0:T(8,128)(2,1)} copy(bf16[4,2,8,128,128]{3,2,4,0,1:T(8,128)(2,1)} %bitcast.204) | data formatting | bytes 4194304 | tf_op jit(solution)/shard_map/transpose | solution.py:84
  111.9 2.0 fusion.45
  113.9 0.8 fusion.30
  115.2 85.4 %all-reduce.3.cloned.1.call-done = (f32[4,16]{1,0:T(4,128)}, f32[4,16,128]{2,1,0:T(8,128)}, f32[4,16,128]{2,1,0:T(8,128)}) async-done(((f32[4,16]{1,0:T(4,128)}, f32[4,16,128]{2,1,0:T(8,128)}, f32[4,16,128]{2,1,0:T(8,128)}), (f32[4,16]{1,0:T(4,128)}, f32[4,16,128]{2,1,0:T(8,128)}, f32[4,16,128]{2,1,0:T(8,128)})) %all-reduce.3.cloned.1.call-update) | async-done | bytes 65808 | tf_op jit(solution)/shard_map/psum | solution.py:110
  200.6 0.8 compare_convert_fusion
  201.4 0.9 fusion.41
  202.3 0.9 fusion.39
  203.3 17.0 %while.33 = (s32[]{:T(128)}, f32[4,4,128]{2,1,0:T(4,128)S(1)}, f32[4,4,128]{2,1,0:T(4,128)S(1)}, f32[4,4,128,128]{3,2,1,0:T(8,128)}, f32[4,4,16]{2,0,1:T(4,128)S...) while((s32[]{:T(128)}, f32[4,4,128]{2,1,0:T(4,128)S(1)}, ...), condition=%wide.region_8.9_spmd, body=%wide.region_5.8_spmd.sunk | while | flops 549325888 | bytes 25776720 | solution.py:55
  203.7 0.9 select_reduce_fusion.2
  204.7 1.1 fusion.85
  205.8 1.7 fusion.86
  208.0 0.9 select_reduce_fusion.2
  208.9 1.1 fusion.85
  210.1 1.7 fusion.86
  212.2 0.9 select_reduce_fusion.2
  213.2 1.1 fusion.85
  214.3 1.7 fusion.86
  216.5 0.9 select_reduce_fusion.2
  217.4 1.1 fusion.85
  218.5 1.7 fusion.86
  220.3 2.3 copy.102
  223.0 23.5 %all_gather.9 = f32[16,4,64,8]{2,3,1,0:T(8,128)S(1)} all-gather(f32[1,4,64,8]{2,3,1,0:T(8,128)S(1)} %copy.99), channel_id=1, replica_groups=mesh['head'=2,'clus'=16] {'clus'}, dimensions={0}, use_global_device_ids=true | all-gather | bytes 139264 | tf_op jit(solution)/shard_map/all_gather | solution.py:17
  246.5 19.5 %all_gather.10 = f32[16,4,64,8]{2,3,1,0:T(8,128)S(1)} all-gather(f32[1,4,64,8]{2,3,1,0:T(8,128)S(1)} %copy.101), channel_id=1, replica_groups=mesh['head'=2,'clus'=16] {'clus'}, dimensions={0}, use_global_device_ids=true | all-gather | bytes 139264 | tf_op jit(solution)/shard_map/all_gather | solution.py:17
  266.1 87.1 %all-gather.2.cloned.1.call-done = f32[16,4,64,8,128]{4,3,2,1,0:T(8,128)} async-done(((f32[1,4,64,8,128]{4,3,2,1,0:T(8,128)}), f32[16,4,64,8,128]{4,3,2,1,0:T(8,128)}) %all-gather.2.cloned.1.call-update) | async-done | bytes 16777232 | tf_op jit(solution)/shard_map/all_gather | solution.py:17
  353.2 1.3 slice_bitcast_fusion
  354.5 32.2 %while.34 = (s32[]{:T(128)}, f32[4,64,8]{1,2,0:T(8,128)S(1)}, f32[4,64,8]{1,2,0:T(8,128)S(1)}, f32[4,64,8,128]{3,2,1,0:T(8,128)S(1)}, f32[16,4,64,8]{2,3,1,0:T(8...) while((s32[]{:T(128)}, f32[4,64,8]{1,2,0:T(8,128)S(1)}, ...), condition=%wide.region_10.11_spmd, body=%wide.region_9.10_spmd.sunk | while | flops 798725 | bytes 3260559 | solution.py:23
  354.7 1.9 fusion.88
  356.9 1.9 fusion.88
  359.0 1.9 fusion.88
  361.1 1.9 fusion.88
  363.3 1.9 fusion.88
  365.4 1.9 fusion.88
  367.6 1.9 fusion.88
  369.7 1.9 fusion.88
  371.9 1.9 fusion.88
  374.0 1.9 fusion.88
  376.2 1.9 fusion.88
  378.3 1.9 fusion.88
  380.4 1.9 fusion.88
  382.6 1.9 fusion.88
  384.7 1.9 fusion.88
  386.9 0.6 copy.132
  (121 shorter events, 7.4 us)
Async XLA Ops:
  30.6 7.2 %copy-start.3 = (s32[4,1,2,8,1]{3,4,2,1,0:T(1,128)S(1)}, s32[4,1,2,8,1]{3,4,2,1,0:T(1,128)}, u32[]{:S(2)}) copy-start(s32[4,1,2,8,1]{3,4,2,1,0:T(1,128)} %param.12) | copy-start | bytes 772
  33.2 34.4 %all-to-all-start = ((bf16[2,2,262144]{2,1,0:T(2,128)(2,1)}), bf16[2,2,262144]{2,1,0:T(2,128)(2,1)S(1)}, u32[]{:S(2)}, u32[]{:S(2)}) async-start(bf16[2,2,262144]{2,1,0:T(2,128)(2,1)} %reshape.74), calls=%async_computation | async-start | bytes 4194304 | tf_op jit(solution)/shard_map/all_to_all | solution.py:75
  49.5 18.0 %copy-start.2 = (s32[4,4,4]{2,1,0:T(4,128)S(1)}, s32[4,4,4]{2,1,0:T(4,128)}, u32[]{:S(2)}) copy-start(s32[4,4,4]{2,1,0:T(4,128)} %param.13) | copy-start | bytes 772
  67.5 30.8 %all-to-all-start.1 = ((bf16[2,2,262144]{2,1,0:T(2,128)(2,1)}), bf16[2,2,262144]{2,1,0:T(2,128)(2,1)}, u32[]{:S(2)}, u32[]{:S(2)}) async-start(bf16[2,2,262144]{2,1,0:T(2,128)(2,1)} %reshape.76), calls=%async_computation.1 | async-start | bytes 4194304 | tf_op jit(solution)/shard_map/all_to_all | solution.py:76
  72.4 128.2 %all-reduce.3.cloned.1.call-start = ((), (), s32[]{:S(2)}) async-start(), calls=%async_computation.3 | async-start | bytes 135168 | tf_op jit(solution)/shard_map/psum | solution.py:110
  107.5 7.5 %copy-start.1 = (bf16[64,4096]{1,0:T(8,128)(2,1)S(1)}, bf16[64,4096]{1,0:T(8,128)(2,1)}, u32[]{:S(2)}) copy-start(bf16[64,4096]{1,0:T(8,128)(2,1)} %param.11) | copy-start | bytes 1572868
  114.6 238.5 %all-gather.2.cloned.1.call-start = ((), (), s32[]{:S(2)}) async-start(), calls=%async_computation.2 | async-start | bytes 17825792 | tf_op jit(solution)/shard_map/all_gather | solution.py:17
  203.7 2.1 copy-start
  208.0 2.1 copy-start
  212.2 2.1 copy-start
  216.4 2.1 copy-start
Sparse Core Ops, SparseCore 0:
  114.8 85.8 all-reduce.2
  222.7 130.4 all-gather.1
where the time goes:
time: 396 us; the launch traced here: 394 us
  waiting for transfers between devices  185 us (47%)
  other arithmetic  62.3 us (16%)
  local copies, waits for them, and re-layouts  62.1 us (16%)
  blocking collectives  43.1 us (11%)
  matrix products  18.3 us (5%)
  between operations  13.6 us (3%)
  starting transfers between devices  9.32 us (2%)
    all_gather x1, waiting for transfers between devices, combined_all(): everything = jax.tree.map(lambda part: lax.all_gather(part, axis), shard)  87.1 us
    psum x1, waiting for transfers between devices, local(): lax.psum((local_keys, local_values, local_counts), 'clus')  85.4 us
    unnamed x20, local copies, waits for them, and re-layouts  47 us
    all_gather x2, blocking collectives, combined_all(): everything = jax.tree.map(lambda part: lax.all_gather(part, axis), shard)  43.1 us
    add x15, other arithmetic, combine_parts(): numer_first * factor_first[..., None]  28.4 us
    unnamed x4, other arithmetic  27.7 us
    all_to_all x1, waiting for transfers between devices, local(): lax.all_to_all(value_cache, 'head', split_axis=2, concat_axis=0, tiled=True)  12.5 us
  transfers between devices with their start and end apart: 4, of which 3 were waited for; matrix products, arithmetic and copies ran while one was open for 11% of the time, Pallas kernels for 0%

commit v1 on v0

--- a/solution.py
+++ b/solution.py
@@ -1,6 +1,11 @@
+import functools
+import math
+
 import jax
 import jax.numpy as jnp
 from jax import lax
+from jax.experimental import pallas as pl
+from jax.experimental.pallas import tpu as pltpu
 from jax.sharding import PartitionSpec as P
 
 DH = 128
@@ -136,6 +141,347 @@
     )
 
 
+MESH = pl.DeviceIdType.MESH
+dead = -1e30
+lowest_top = -1e9
+log2_scale = math.log2(math.e) * DH**-0.5
+nt = (((1,), (1,)), ((), ()))
+
+
+def fast_kernel(
+    k_hbm, v_hbm, q_ref, bt_ref, a_ref, ab_ref, out_ref,
+    kbuf, vbuf, qx, btx, ax, bias, o_buf, st_buf, o_rx, st_rx,
+    ts_buf, ts_rx, cs_buf, cs_rx, red_buf, tot_rx, wt,
+    loc_sem, kv_send, kv_recv, in_send, in_recv,
+    o_send, o_recv, st_send, st_recv, ts_sem, cs_send, cs_recv, tot_send, tot_recv,
+):
+    x, i = lax.axis_index("head"), lax.axis_index("clus")
+    clus = lax.axis_size("clus")
+    chips = clus // 2
+    c, w = lax.rem(i, 2), i // 2
+    sib = i + 1 - 2 * c
+    slot = x * chips + w
+    rows = k_hbm.shape[0]
+    tiles = rows // TILE
+    count = float(clus * TILE)
+    me = x * clus + i
+
+    def pair_of(half, core):
+        return 2 * (x if half == 0 else 1 - x) + core
+
+    def kv_copies(half, remote):
+        copies = []
+        for hh in range(2):
+            for n, (src, dst) in enumerate(((k_hbm, kbuf), (v_hbm, vbuf))):
+                number = half * 4 + hh * 2 + n
+                pair = pair_of(half, 1 - c if remote else c)
+                column = pl.ds(pl.multiple_of((pair * 2 + hh) * DH, DH), DH)
+                if remote:
+                    copies.append(pltpu.make_async_remote_copy(
+                        src_ref=src.at[:, column], dst_ref=dst.at[half, hh, pl.ds(rows, rows)],
+                        send_sem=kv_send.at[number], recv_sem=kv_recv.at[number],
+                        device_id=(x, sib), device_id_type=MESH))
+                else:
+                    copies.append(pltpu.make_async_copy(
+                        src.at[:, column], dst.at[half, hh, pl.ds(0, rows)], loc_sem.at[number]))
+        return copies
+
+    def remote(src, dst, send_sem, recv_sem, device):
+        return pltpu.make_async_remote_copy(
+            src_ref=src, dst_ref=dst, send_sem=send_sem, recv_sem=recv_sem,
+            device_id=device, device_id_type=MESH)
+
+    own_kv = [kv_copies(0, False), kv_copies(1, False)]
+    far_kv = [kv_copies(0, True), kv_copies(1, True)]
+    for copy in own_kv[0] + own_kv[1]:
+        copy.start()
+
+    barrier = pltpu.get_barrier_semaphore()
+
+    def greet(k, carry):
+        other = lax.rem(me + k, 2 * clus)
+        pl.semaphore_signal(
+            barrier, inc=1, device_id=(other // clus, lax.rem(other, clus)), device_id_type=MESH)
+        return carry
+
+    lax.fori_loop(1, 2 * clus, greet, 0)
+    pl.semaphore_wait(barrier, 2 * clus - 1)
+
+    small = [
+        remote(bt_ref.at[0, 1], btx.at[0], in_send.at[0], in_recv.at[0], (x, sib)),
+        remote(bt_ref.at[1, 0], btx.at[1], in_send.at[1], in_recv.at[1], (1 - x, i)),
+        remote(bt_ref.at[1, 1], btx.at[2], in_send.at[2], in_recv.at[2], (1 - x, sib)),
+        remote(a_ref.at[1], ax, in_send.at[3], in_recv.at[3], (x, sib)),
+        remote(q_ref.at[pl.ds(2 * c, 2)], qx, in_send.at[4], in_recv.at[4], (1 - x, i)),
+    ]
+    for copy in small[:3] + far_kv[0] + small[4:] + small[3:4] + far_kv[1]:
+        copy.start()
+
+    def spread(table):
+        return jnp.concatenate(
+            [jnp.broadcast_to(table[:, t : t + 1], (table.shape[0], TILE)) for t in range(tiles)],
+            axis=1)
+
+    def parts_for(half, b, j):
+        dest = b * 4 + j
+        device = ((x if half == 0 else 1 - x), dest)
+        return dest, device, (
+            (o_buf.at[half, dest], o_rx.at[c, slot], o_send.at[half, dest], o_recv.at[c, slot]),
+            (st_buf.at[half, b], st_rx.at[c, slot], st_send.at[half, dest], st_recv.at[c, slot]),
+        )
+
+    square = lax.broadcasted_iota(jnp.int32, (128, 128), 0) == lax.broadcasted_iota(
+        jnp.int32, (128, 128), 1)
+
+    def as_row(column):
+        return jnp.sum(jnp.where(square, column, 0.0), axis=0, keepdims=True)
+
+    def attend(half, b, carry):
+        stats = []
+        for hh in range(2):
+            span = pl.ds(pl.multiple_of(b * 128, 128), 128)
+            queries = q_ref[2 * c + hh, span, :] if half == 0 else qx[hh, span, :]
+            scores = lax.dot_general(
+                queries, kbuf[half, hh], nt, preferred_element_type=jnp.float32)
+            scores = scores * log2_scale + bias[half, pl.ds(hh * 4 + b, 1), :]
+            top = jnp.maximum(jnp.max(scores, axis=1, keepdims=True), lowest_top)
+            weights = jnp.exp2(scores - top)
+            total = jnp.sum(weights, axis=1, keepdims=True)
+            numer = jnp.dot(
+                weights.astype(jnp.bfloat16), vbuf[half, hh], preferred_element_type=jnp.float32)
+            numer = numer.astype(jnp.bfloat16)
+            for j in range(4):
+                o_buf[half, b * 4 + j, hh] = numer[32 * j : 32 * (j + 1)]
+            stats += [as_row(top), as_row(total)]
+        st_buf[half, b] = jnp.concatenate(stats + [jnp.zeros((4, 128), jnp.float32)], axis=0)
+        for j in range(4):
+            dest, device, parts = parts_for(half, b, j)
+
+            @pl.when((dest != i) if half == 0 else (dest >= 0))
+            def _():
+                for src, dst, send_sem, recv_sem in parts:
+                    remote(src, dst, send_sem, recv_sem, device).start()
+
+            if half == 0:
+                @pl.when(dest == i)
+                def _():
+                    for src, dst, send_sem, recv_sem in parts:
+                        pltpu.make_async_copy(src, dst, recv_sem).start()
+        return carry
+
+    for copy in own_kv[0]:
+        copy.wait()
+    small[0].wait_recv()
+    for copy in far_kv[0]:
+        copy.wait_recv()
+    bias[0] = jnp.concatenate([spread(bt_ref[0, 0]), spread(btx[0])], axis=1)
+    lax.fori_loop(0, 4, functools.partial(attend, 0), 0)
+
+    for copy in own_kv[1]:
+        copy.wait()
+    for copy in far_kv[1] + [small[1], small[2], small[3], small[4]]:
+        copy.wait_recv()
+    bias[1] = jnp.concatenate([spread(btx[1]), spread(btx[2])], axis=1)
+
+    tile_rows = lax.broadcasted_iota(jnp.int32, (2 * tiles, 2 * rows), 0)
+    tile_cols = lax.broadcasted_iota(jnp.int32, (2 * tiles, 2 * rows), 1) // TILE
+    unit = jnp.where(tile_rows == tile_cols, 1.0, 0.0).astype(jnp.bfloat16)
+    for half in (1, 0):
+        for n, buf in enumerate((kbuf, vbuf)):
+            for hh in range(2):
+                sums = jnp.dot(unit, buf[half, hh], preferred_element_type=jnp.float32)
+                ts_buf[half, n, hh] = sums.reshape(2, tiles, DH)
+    ts_copy = remote(ts_buf.at[1], ts_rx, ts_sem.at[0], ts_sem.at[1], (1 - x, i))
+    ts_copy.start()
+
+    lax.fori_loop(0, 2, functools.partial(attend, 1), 0)
+
+    ts_copy.wait_recv()
+    all_sums = jnp.concatenate(
+        [ts_buf[0].reshape(8, tiles, DH), ts_rx[...].reshape(8, tiles, DH)], axis=1
+    ).reshape(16 * tiles, DH)
+    clustered = jnp.dot(
+        a_ref[0] + ax[...], all_sums, precision=highest, preferred_element_type=jnp.float32)
+    cs_buf[...] = clustered.reshape(chips, 8, DH)
+    cs_rx[w] = cs_buf[w]
+
+    def cs_out(k):
+        chip = lax.rem(w + k, chips)
+        return remote(
+            cs_buf.at[chip], cs_rx.at[w], cs_send.at[chip], cs_recv.at[w], (x, 2 * chip + c))
+
+    def cs_in(k):
+        chip = lax.rem(w + k, chips)
+        return remote(
+            cs_buf.at[chip], cs_rx.at[chip], cs_send.at[chip], cs_recv.at[chip], (x, 2 * chip + c))
+
+    for k in range(1, chips):
+        cs_out(k).start()
+
+    lax.fori_loop(2, 4, functools.partial(attend, 1), 0)
+
+    for k in range(1, chips):
+        cs_in(k).wait_recv()
+    reduced = jnp.sum(cs_rx[...], axis=0)
+    red_buf[...] = reduced
+    tot_rx[c, w] = reduced
+
+    def tot_out(k):
+        other = lax.rem(i + k, clus)
+        return remote(
+            red_buf, tot_rx.at[c, w], tot_send.at[other], tot_recv.at[i], (x, other))
+
+    def tot_in(k):
+        other = lax.rem(i + k, clus)
+        return remote(
+            red_buf, tot_rx.at[lax.rem(other, 2), other // 2], tot_send.at[other],
+            tot_recv.at[other], (x, other))
+
+    for k in range(1, clus):
+        tot_out(k).start()
+    for k in range(1, clus):
+        tot_in(k).wait_recv()
+
+    def arrive(n, carry):
+        core, source = n // clus, lax.rem(n, clus)
+        remote(o_buf.at[0, 0], o_rx.at[core, source], o_send.at[0, 0],
+               o_recv.at[core, source], (x, sib)).wait_recv()
+        remote(st_buf.at[0, 0], st_rx.at[core, source], st_send.at[0, 0],
+               st_recv.at[core, source], (x, sib)).wait_recv()
+        return carry
+
+    lax.fori_loop(0, 2 * clus, arrive, 0)
+
+    block, part = i // 4, lax.rem(i, 4)
+    for h in range(4):
+        p, hh = h // 2, h % 2
+        totals = tot_rx[p].reshape(chips * 8, DH)
+        queries = q_ref[h, pl.ds(pl.multiple_of(block * 128, 128), 128), :].astype(jnp.float32)
+        approx = lax.dot_general(
+            totals, queries, nt, precision=highest, preferred_element_type=jnp.float32)
+        approx = approx * (log2_scale / count) + ab_ref[h]
+        tops, sums = st_rx[p, :, 2 * hh, :], st_rx[p, :, 2 * hh + 1, :]
+        top = jnp.maximum(
+            jnp.max(tops, axis=0, keepdims=True), jnp.max(approx, axis=0, keepdims=True))
+        factor = jnp.exp2(tops - top)
+        approx_weight = jnp.exp2(approx - top)
+        total = jnp.sum(factor * sums, axis=0, keepdims=True) + count * jnp.sum(
+            approx_weight, axis=0, keepdims=True)
+        inverse = 1.0 / total
+        mixed = jnp.concatenate(
+            [factor * inverse, jnp.zeros((48, 128), jnp.float32),
+             pltpu.roll(approx_weight * inverse, 4, 0)], axis=0)
+        wt[...] = mixed.T
+        mine = wt[pl.ds(pl.multiple_of(part * 32, 32), 32), :]
+        numer = jnp.dot(
+            mine, jnp.concatenate([jnp.zeros((64, DH), jnp.float32), totals], axis=0),
+            precision=highest, preferred_element_type=jnp.float32)
+        for source in range(2 * chips):
+            numer = numer + mine[:, source : source + 1] * o_rx[p, source, hh].astype(jnp.float32)
+        out_ref[h] = numer.astype(jnp.bfloat16)
+
+    for copy in small + far_kv[0] + far_kv[1] + [ts_copy]:
+        copy.wait_send()
+    for k in range(1, chips):
+        cs_out(k).wait_send()
+    for k in range(1, clus):
+        tot_out(k).wait_send()
+
+    def sent(dest, carry):
+        for half in range(2):
+            @pl.when((dest != i) if half == 0 else (dest >= 0))
+            def _():
+                _, device, parts = parts_for(half, dest // 4, lax.rem(dest, 4))
+                for src, dst, send_sem, recv_sem in parts:
+                    remote(src, dst, send_sem, recv_sem, device).wait_send()
+        return carry
+
+    lax.fori_loop(0, clus, sent, 0)
+
+
+def fast_local(key_cache, value_cache, prompt_queries, tile_cluster, listed_clusters):
+    clus = lax.axis_size("clus")
+    x, i = lax.axis_index("head"), lax.axis_index("clus")
+    c = lax.rem(i, 2)
+    _, rows, width = key_cache.shape
+    tiles = rows // TILE
+    chips = clus // 2
+    query_count = prompt_queries.shape[0]
+    heads = prompt_queries.shape[1] // (GROUP * DH)
+    blocks = query_count // QBLK
+    queries = prompt_queries.reshape(query_count, heads, GROUP, DH).transpose(1, 0, 2, 3)
+    queries = queries.reshape(heads, query_count * GROUP, DH)
+
+    ids = tile_cluster.reshape(2, 2, 2, tiles)
+    ids = jnp.where(x == 0, ids, ids[:, :, ::-1])
+    ids = jnp.where(c == 0, ids, ids[::-1])
+    listed = listed_clusters.reshape(2, 2, blocks, -1)
+    listed_mine = jnp.where(c == 0, listed, listed[::-1])
+    live = jnp.any(
+        ids[:, :, :, None, :, None] == listed_mine[:, :, None, :, None, :], axis=-1)
+    tables = jnp.where(live, 0.0, dead).transpose(2, 0, 1, 3, 4).reshape(2, 2, 2 * blocks, tiles)
+    tables = jnp.pad(tables, ((0, 0), (0, 0), (0, 0), (0, 128 - tiles)))
+
+    r = jnp.arange(8 * chips, dtype=jnp.int32)
+    number, kv_r, hh_r = 2 * (r // 8) + r % 2, (r // 4) % 2, (r // 2) % 2
+    k = jnp.arange(16 * tiles, dtype=jnp.int32)
+    kv_k, hh_k, side_k = k // (8 * tiles), (k // (4 * tiles)) % 2, (k // (2 * tiles)) % 2
+    same = (kv_r[:, None] == kv_k[None, :]) & (hh_r[:, None] == hh_k[None, :])
+    named = jnp.broadcast_to(
+        ids.reshape(2, 1, 2, 1, 2 * tiles), (2, 2, 2, 2, 2 * tiles)).reshape(2, 1, 16 * tiles)
+    side = jnp.arange(2, dtype=jnp.int32)[:, None, None]
+    member = (named == number[None, :, None]) & same[None] & (side_k[None, None, :] == side)
+    member = member.astype(jnp.float32)
+
+    listed_here = lax.dynamic_index_in_dim(
+        listed_clusters, i * blocks // clus, 1, keepdims=False)
+    skipped = jnp.any(listed_here[:, :, None] == number, axis=1)
+    usable = (kv_r == 0)[None] & (hh_r[None] == (jnp.arange(heads) % 2)[:, None]) & ~skipped
+    approx_bias = jnp.broadcast_to(
+        jnp.where(usable, 0.0, dead)[:, :, None], (heads, 8 * chips, 128))
+
+    dma = pltpu.SemaphoreType.DMA
+    f32, bf16 = jnp.float32, jnp.bfloat16
+    share = query_count * GROUP // clus
+    vmem = pl.BlockSpec(memory_space=pltpu.VMEM)
+    anywhere = pl.BlockSpec(memory_space=pl.ANY)
+    out = pl.pallas_call(
+        fast_kernel,
+        out_shape=jax.ShapeDtypeStruct((heads, share, DH), bf16),
+        in_specs=[anywhere, anywhere, vmem, vmem, vmem, vmem],
+        out_specs=vmem,
+        scratch_shapes=[
+            pltpu.VMEM((2, 2, 2 * rows, DH), bf16),
+            pltpu.VMEM((2, 2, 2 * rows, DH), bf16),
+            pltpu.VMEM((2, query_count * GROUP, DH), bf16),
+            pltpu.VMEM((3, 2 * blocks, 128), f32),
+            pltpu.VMEM((8 * chips, 16 * tiles), f32),
+            pltpu.VMEM((2, 2 * blocks, 2 * rows), f32),
+            pltpu.VMEM((2, clus, 2, share, DH), bf16),
+            pltpu.VMEM((2, blocks, 8, 128), f32),
+            pltpu.VMEM((2, clus, 2, share, DH), bf16),
+            pltpu.VMEM((2, clus, 8, 128), f32),
+            pltpu.VMEM((2, 2, 2, 2, tiles, DH), f32),
+            pltpu.VMEM((2, 2, 2, tiles, DH), f32),
+            pltpu.VMEM((chips, 8, DH), f32),
+            pltpu.VMEM((chips, 8, DH), f32),
+            pltpu.VMEM((8, DH), f32),
+            pltpu.VMEM((2, chips, 8, DH), f32),
+            pltpu.VMEM((128, 128), f32),
+            dma((8,)), dma((8,)), dma((8,)), dma((5,)), dma((5,)),
+            dma((2, clus)), dma((2, clus)), dma((2, clus)), dma((2, clus)),
+            dma((2,)), dma((chips,)), dma((chips,)), dma((clus,)), dma((clus,)),
+        ],
+        compiler_params=pltpu.CompilerParams(
+            collective_id=0, has_side_effects=True, vmem_limit_bytes=48 * 1024 * 1024),
+    )(
+        key_cache.reshape(rows, width), value_cache.reshape(rows, width),
+        queries, tables, member, approx_bias,
+    )
+    out = out.reshape(heads, query_count // clus, GROUP, DH).transpose(1, 0, 2, 3)
+    return out.reshape(query_count // clus, heads * GROUP * DH)
+
+
 def solution(mesh):
     placed = (
         P("head", "clus", None),
@@ -144,6 +490,11 @@
         P("head", "clus", None, None, None),
         P("head", None, None),
     )
+    fits = mesh.shape["head"] == 2 and mesh.shape["clus"] == 16
     return jax.shard_map(
-        local, mesh=mesh, in_specs=placed, out_specs=P("clus", "head"), check_vma=False
-    )
+        fast_local if fits else local,
+        mesh=mesh,
+        in_specs=placed,
+        out_specs=P("clus", "head"),
+        check_vma=False,
+    )

time: 396 us -> 42.4 us (0.11)
  waiting for transfers between devices: 185 us -> 0 us
  other arithmetic: 62.3 us -> 0.52 us
  local copies, waits for them, and re-layouts: 62.1 us -> 3.93 us
  blocking collectives: 43.1 us -> 0 us
  Pallas kernels: 0 us -> 37.6 us
  matrix products: 18.3 us -> 0 us
  between operations: 13.6 us -> 0.2 us
  starting transfers between devices: 9.32 us -> 0 us
    all_gather x1 -> x0, waiting for transfers between devices: 87.1 us -> none  [combined_all(): everything = jax.tree.map(lambda part: lax.all_gather(part, axis), shard)]
    psum x1 -> x0, waiting for transfers between devices: 85.4 us -> none  [local(): lax.psum((local_keys, local_values, local_counts), 'clus')]
    unnamed x20 -> x11, local copies, waits for them, and re-layouts: 47 us -> 3.52 us
    all_gather x2 -> x0, blocking collectives: 43.1 us -> none  [combined_all(): everything = jax.tree.map(lambda part: lax.all_gather(part, axis), shard)]
    pallas_call x0 -> x1, Pallas kernels: none -> 37.6 us  [fast_local(): pl.pallas_call(fast_kernel, out_shape=jax.ShapeDtypeStruct((heads, share,...]
    add x30 -> x1, other arithmetic: 28.8 us -> 0.01 us  [fast_local(): number, kv_r, hh_r = (2 * (r // 8) + r % 2, r // 4 % 2, r // 2 % 2)]
    unnamed x4 -> x0, other arithmetic: 27.7 us -> none
    dot_general x21 -> x0, matrix products: 18.3 us -> none  [the longest x4 6.85 us: one_block(): jnp.dot(probabilities, value_rows, preferred_element_type=jnp.float32)]
  transfers between devices with their start and end apart: 4 -> 0, of which waited for: 3 -> 0; matrix products, arithmetic and copies ran while one was open for 11% -> 0% of each run, Pallas kernels for 0% -> 0%
where the time goes in v1:
time: 42.4 us; the launch traced here: 42.3 us
  Pallas kernels  37.6 us (89%)
  local copies, waits for them, and re-layouts  3.93 us (9%)
  other arithmetic  0.52 us (1%)
    pallas_call x1, Pallas kernels, fast_local(): pl.pallas_call(fast_kernel, out_shape=jax.ShapeDtypeStruct((heads, share,...  37.6 us
    unnamed x11, local copies, waits for them, and re-layouts  3.52 us

profile of v1, /device:TPU:0, one launch (start us, length us, event | category | flops | bytes accessed | tf_op | source)
XLA Modules:
  0.0 42.3 jit_solution(5500258752478179534)
XLA Ops:
  0.0 0.0 copy-start
  0.0 0.0 copy-start.3
  0.0 0.0 copy-start.2
  0.0 1.3 %copy.11 = bf16[8,8,32,128]{3,2,1,0:T(8,128)(2,1)S(1)} copy(bf16[8,8,32,128]{3,1,2,0:T(8,128)(2,1)} %bitcast.31) | data formatting | bytes 1048576
  1.3 0.1 copy.16
  1.4 0.0 copy-done.3
  1.4 0.0 copy-done.2
  1.5 0.1 compare_reduce_fusion
  1.7 0.1 broadcast_in_dim.22
  1.8 0.1 eq.141
  1.9 0.1 compare_and_fusion
  2.0 0.1 and_convert_fusion.a_ref
  2.1 0.1 compare_reduce_fusion.1
  2.2 0.1 and_select_fusion
  2.3 0.1 broadcast_in_dim.28.ab_ref
  2.4 0.0 copy-done
  2.4 0.0 copy-start.1
  2.4 1.6 %copy-done.1 = bf16[1,1024,1024]{2,1,0:T(8,128)(2,1)S(1)} copy-done((bf16[1,1024,1024]{2,1,0:T(8,128)(2,1)S(1)}, bf16[1,1024,1024]{2,1,0:T(8,128)(2,1)}, u32[]{:S(2)}) %copy-start.1) | copy-done | bytes 2097176
  4.0 37.6 %shard_map.55 = bf16[4,32,128]{2,1,0:T(8,128)(2,1)S(1)} custom-call(bf16[1024,1024]{1,0:T(8,128)(2,1)S(1)} %bitcast.28, bf16[1024,1024]{1,0:T(8,128)(2,1)S(1)} %bitcast.29, bf16[4,512,128]{2,1,0:T(8,128)(2,1)S(1)} %bitcast.27, f32[2,2,8,128]{3,2,1,0:T(8,128)S(1)} %pad.4.bt_ref, f32[2,64,128]{2,1,0:T(8,128)S(1)} %and_convert_fusion.a_ref, ...), custom_call_target="tpu_custom_call" | custom-call | tf_op jit(solution)/shard_map/pallas_call | solution.py:448
  41.6 0.6 %copy.17 = bf16[1,4,32,128]{3,1,2,0:T(4,128)(2,1)} copy(bf16[1,4,32,128]{3,2,1,0:T(8,128)(2,1)S(1)} %copy_bitcast_fusion.2) | data formatting | bytes 65536
  (17 shorter events, 0.1 us)
Async XLA Ops:
  0.0 2.4 %copy-start = (bf16[1,1024,1024]{2,1,0:T(8,128)(2,1)S(1)}, bf16[1,1024,1024]{2,1,0:T(8,128)(2,1)}, u32[]{:S(2)}) copy-start(bf16[1,1024,1024]{2,1,0:T(8,128)(2,1)} %param.5) | copy-start | bytes 6291460
  0.0 1.4 %copy-start.3 = (s32[4,4,4]{2,1,0:T(4,128)S(1)}, s32[4,4,4]{2,1,0:T(4,128)}, u32[]{:S(2)}) copy-start(s32[4,4,4]{2,1,0:T(4,128)} %param.9) | copy-start | bytes 772
  0.0 1.4 %copy-start.2 = (s32[4,1,2,8,1]{3,4,2,1,0:T(1,128)S(1)}, s32[4,1,2,8,1]{3,4,2,1,0:T(1,128)}, u32[]{:S(2)}) copy-start(s32[4,1,2,8,1]{3,4,2,1,0:T(1,128)} %param.8) | copy-start | bytes 772
  2.4 1.6 %copy-start.1 = (bf16[1,1024,1024]{2,1,0:T(8,128)(2,1)S(1)}, bf16[1,1024,1024]{2,1,0:T(8,128)(2,1)}, u32[]{:S(2)}) copy-start(bf16[1,1024,1024]{2,1,0:T(8,128)(2,1)} %param.6) | copy-start | bytes 6291460

commit v2 on v1

--- a/solution.py
+++ b/solution.py
@@ -150,8 +150,8 @@
 
 def fast_kernel(
     k_hbm, v_hbm, q_ref, bt_ref, a_ref, ab_ref, out_ref,
-    kbuf, vbuf, qx, btx, ax, bias, o_buf, st_buf, o_rx, st_rx,
-    ts_buf, ts_rx, cs_buf, cs_rx, red_buf, tot_rx, wt,
+    kbuf, vbuf, qx, qall, btx, ax, bias, o_buf, st_buf, o_rx, st_rx,
+    ts_buf, ts_rx, cs_buf, cs_rx, red_buf, tot_rx, wt, hot_ref,
     loc_sem, kv_send, kv_recv, in_send, in_recv,
     o_send, o_recv, st_send, st_recv, ts_sem, cs_send, cs_recv, tot_send, tot_recv,
 ):
@@ -165,6 +165,8 @@
     tiles = rows // TILE
     count = float(clus * TILE)
     me = x * clus + i
+    wide = GROUP * DH
+    span = 2 * QBLK * GROUP
 
     def pair_of(half, core):
         return 2 * (x if half == 0 else 1 - x) + core
@@ -212,22 +214,23 @@
         remote(bt_ref.at[1, 0], btx.at[1], in_send.at[1], in_recv.at[1], (1 - x, i)),
         remote(bt_ref.at[1, 1], btx.at[2], in_send.at[2], in_recv.at[2], (1 - x, sib)),
         remote(a_ref.at[1], ax, in_send.at[3], in_recv.at[3], (x, sib)),
-        remote(q_ref.at[pl.ds(2 * c, 2)], qx, in_send.at[4], in_recv.at[4], (1 - x, i)),
+        remote(q_ref.at[:, pl.ds(pl.multiple_of(c * 2 * wide, 128), 2 * wide)], qx,
+               in_send.at[4], in_recv.at[4], (1 - x, i)),
     ]
     for copy in small[:3] + far_kv[0] + small[4:] + small[3:4] + far_kv[1]:
         copy.start()
 
-    def spread(table):
-        return jnp.concatenate(
-            [jnp.broadcast_to(table[:, t : t + 1], (table.shape[0], TILE)) for t in range(tiles)],
-            axis=1)
-
-    def parts_for(half, b, j):
-        dest = b * 4 + j
-        device = ((x if half == 0 else 1 - x), dest)
-        return dest, device, (
+    def regroup(rows_in):
+        count_in = rows_in.shape[0]
+        split = rows_in.astype(jnp.float32).reshape(count_in, GROUP, DH)
+        return split.reshape(count_in * GROUP, DH).astype(jnp.bfloat16)
+
+    def parts_for(half, dest):
+        device = (x + half * (1 - 2 * x), dest)
+        return device, (
             (o_buf.at[half, dest], o_rx.at[c, slot], o_send.at[half, dest], o_recv.at[c, slot]),
-            (st_buf.at[half, b], st_rx.at[c, slot], st_send.at[half, dest], st_recv.at[c, slot]),
+            (st_buf.at[half, dest // 4], st_rx.at[c, slot], st_send.at[half, dest],
+             st_recv.at[c, slot]),
         )
 
     square = lax.broadcasted_iota(jnp.int32, (128, 128), 0) == lax.broadcasted_iota(
@@ -236,74 +239,111 @@
     def as_row(column):
         return jnp.sum(jnp.where(square, column, 0.0), axis=0, keepdims=True)
 
-    def attend(half, b, carry):
-        stats = []
-        for hh in range(2):
-            span = pl.ds(pl.multiple_of(b * 128, 128), 128)
-            queries = q_ref[2 * c + hh, span, :] if half == 0 else qx[hh, span, :]
-            scores = lax.dot_general(
-                queries, kbuf[half, hh], nt, preferred_element_type=jnp.float32)
-            scores = scores * log2_scale + bias[half, pl.ds(hh * 4 + b, 1), :]
-            top = jnp.maximum(jnp.max(scores, axis=1, keepdims=True), lowest_top)
-            weights = jnp.exp2(scores - top)
-            total = jnp.sum(weights, axis=1, keepdims=True)
-            numer = jnp.dot(
-                weights.astype(jnp.bfloat16), vbuf[half, hh], preferred_element_type=jnp.float32)
-            numer = numer.astype(jnp.bfloat16)
+    key_tile = lax.broadcasted_iota(jnp.int32, (2 * rows, 128), 0) // TILE
+    hot = key_tile == lax.broadcasted_iota(jnp.int32, (2 * rows, 128), 1)
+    hot_ref[...] = jnp.where(hot, 1.0, 0.0).astype(jnp.bfloat16)
+    st_buf[...] = jnp.zeros_like(st_buf)
+
+    def attend(half, pair, hh):
+        start = pl.multiple_of(pair * span, span)
+        masks = [
+            jnp.broadcast_to(bias[half, pl.ds(hh * 4 + pair * 2 + n, 1), :], (128, 128))
+            for n in range(2)
+        ]
+        masks = jnp.concatenate(masks, axis=0).astype(jnp.bfloat16)
+        queries = jnp.concatenate([qall[half, hh, pl.ds(start, span), :], masks], axis=1)
+        keys = jnp.concatenate([kbuf[half, hh], hot_ref[...]], axis=1)
+        scores = lax.dot_general(queries, keys, nt, preferred_element_type=jnp.float32)
+        top = jnp.maximum(jnp.max(scores, axis=1, keepdims=True), lowest_top) * log2_scale
+        weights = jnp.exp2(scores * log2_scale - top).astype(jnp.bfloat16)
+        values = jnp.concatenate(
+            [vbuf[half, hh], jnp.ones((2 * rows, 128), jnp.bfloat16)], axis=1)
+        numer = jnp.dot(weights, values, preferred_element_type=jnp.float32)
+        for n in range(2):
+            block = pair * 2 + n
+            part = slice(128 * n, 128 * (n + 1))
+            st_buf[half, block, pl.ds(hh * 2, 1), :] = as_row(top[part])
+            st_buf[half, block, pl.ds(hh * 2 + 1, 1), :] = as_row(numer[part, DH:])
             for j in range(4):
-                o_buf[half, b * 4 + j, hh] = numer[32 * j : 32 * (j + 1)]
-            stats += [as_row(top), as_row(total)]
-        st_buf[half, b] = jnp.concatenate(stats + [jnp.zeros((4, 128), jnp.float32)], axis=0)
-        for j in range(4):
-            dest, device, parts = parts_for(half, b, j)
-
-            @pl.when((dest != i) if half == 0 else (dest >= 0))
-            def _():
-                for src, dst, send_sem, recv_sem in parts:
-                    remote(src, dst, send_sem, recv_sem, device).start()
-
-            if half == 0:
-                @pl.when(dest == i)
+                first = 128 * n + 32 * j
+                o_buf[half, block * 4 + j, hh] = numer[first : first + 32, :DH].astype(
+                    jnp.bfloat16)
+
+    def ship(half, dest):
+        device, parts = parts_for(half, dest)
+        here = (half == 0) & (dest == i)
+
+        @pl.when(jnp.logical_not(here))
+        def _():
+            for src, dst, send_sem, recv_sem in parts:
+                remote(src, dst, send_sem, recv_sem, device).start()
+
+        @pl.when(here)
+        def _():
+            for src, dst, send_sem, recv_sem in parts:
+                pltpu.make_async_copy(src, dst, recv_sem).start()
+
+    def place_queries(half, source, first):
+        def block_of(n, carry):
+            hh, block = n // 4, lax.rem(n, 4)
+            for head in range(2):
+                @pl.when(hh == head)
                 def _():
-                    for src, dst, send_sem, recv_sem in parts:
-                        pltpu.make_async_copy(src, dst, recv_sem).start()
-        return carry
-
-    for copy in own_kv[0]:
-        copy.wait()
-    small[0].wait_recv()
-    for copy in far_kv[0]:
-        copy.wait_recv()
-    bias[0] = jnp.concatenate([spread(bt_ref[0, 0]), spread(btx[0])], axis=1)
-    lax.fori_loop(0, 4, functools.partial(attend, 0), 0)
-
-    for copy in own_kv[1]:
-        copy.wait()
-    for copy in far_kv[1] + [small[1], small[2], small[3], small[4]]:
-        copy.wait_recv()
-    bias[1] = jnp.concatenate([spread(btx[1]), spread(btx[2])], axis=1)
-
-    tile_rows = lax.broadcasted_iota(jnp.int32, (2 * tiles, 2 * rows), 0)
-    tile_cols = lax.broadcasted_iota(jnp.int32, (2 * tiles, 2 * rows), 1) // TILE
-    unit = jnp.where(tile_rows == tile_cols, 1.0, 0.0).astype(jnp.bfloat16)
-    for half in (1, 0):
-        for n, buf in enumerate((kbuf, vbuf)):
-            for hh in range(2):
-                sums = jnp.dot(unit, buf[half, hh], preferred_element_type=jnp.float32)
-                ts_buf[half, n, hh] = sums.reshape(2, tiles, DH)
+                    columns = pl.ds(pl.multiple_of(first + head * wide, 128), wide)
+                    taken = source[pl.ds(pl.multiple_of(block * QBLK, QBLK), QBLK), columns]
+                    qall[half, head, pl.ds(pl.multiple_of(block * 128, 128), 128), :] = regroup(
+                        taken)
+            return carry
+
+        lax.fori_loop(0, 8, block_of, 0)
+
+    def first_half():
+        for copy in own_kv[0]:
+            copy.wait()
+        place_queries(0, q_ref, c * 2 * wide)
+        small[0].wait_recv()
+        for copy in far_kv[0]:
+            copy.wait_recv()
+        bias[0] = bt_ref[0, 0] + btx[0]
+
+    def tile_sums():
+        for copy in own_kv[1]:
+            copy.wait()
+        for copy in far_kv[1]:
+            copy.wait_recv()
+
+        def add_up(n, carry):
+            half, hh = n // 2, lax.rem(n, 2)
+            for m, buf in enumerate((kbuf, vbuf)):
+                for side in range(2):
+                    part = buf[half, hh, side * rows : (side + 1) * rows]
+                    ts_buf[half, m, hh, side] = jnp.sum(
+                        part.astype(jnp.float32).reshape(tiles, TILE, DH), axis=1)
+            return carry
+
+        lax.fori_loop(0, 4, add_up, 0)
+        ts_copy.start()
+
+    def second_half():
+        for copy in [small[1], small[2], small[4]]:
+            copy.wait_recv()
+        place_queries(1, qx, 0)
+        bias[1] = btx[1] + btx[2]
+
     ts_copy = remote(ts_buf.at[1], ts_rx, ts_sem.at[0], ts_sem.at[1], (1 - x, i))
-    ts_copy.start()
-
-    lax.fori_loop(0, 2, functools.partial(attend, 1), 0)
-
-    ts_copy.wait_recv()
-    all_sums = jnp.concatenate(
-        [ts_buf[0].reshape(8, tiles, DH), ts_rx[...].reshape(8, tiles, DH)], axis=1
-    ).reshape(16 * tiles, DH)
-    clustered = jnp.dot(
-        a_ref[0] + ax[...], all_sums, precision=highest, preferred_element_type=jnp.float32)
-    cs_buf[...] = clustered.reshape(chips, 8, DH)
-    cs_rx[w] = cs_buf[w]
+
+    def cluster_sums():
+        small[3].wait_recv()
+        ts_copy.wait_recv()
+        all_sums = jnp.concatenate(
+            [ts_buf[0].reshape(8, tiles, DH), ts_rx[...].reshape(8, tiles, DH)], axis=1
+        ).reshape(16 * tiles, DH)
+        clustered = jnp.dot(
+            a_ref[0] + ax[...], all_sums, precision=highest, preferred_element_type=jnp.float32)
+        cs_buf[...] = clustered.reshape(chips, 8, DH)
+        cs_rx[w] = cs_buf[w]
+        for k in range(1, chips):
+            cs_out(k).start()
 
     def cs_out(k):
         chip = lax.rem(w + k, chips)
@@ -315,16 +355,14 @@
         return remote(
             cs_buf.at[chip], cs_rx.at[chip], cs_send.at[chip], cs_recv.at[chip], (x, 2 * chip + c))
 
-    for k in range(1, chips):
-        cs_out(k).start()
-
-    lax.fori_loop(2, 4, functools.partial(attend, 1), 0)
-
-    for k in range(1, chips):
-        cs_in(k).wait_recv()
-    reduced = jnp.sum(cs_rx[...], axis=0)
-    red_buf[...] = reduced
-    tot_rx[c, w] = reduced
+    def reduce_sums():
+        for k in range(1, chips):
+            cs_in(k).wait_recv()
+        reduced = jnp.sum(cs_rx[...], axis=0)
+        red_buf[...] = reduced
+        tot_rx[c, w] = reduced
+        for k in range(1, clus):
+            tot_out(k).start()
 
     def tot_out(k):
         other = lax.rem(i + k, clus)
@@ -337,8 +375,30 @@
             red_buf, tot_rx.at[lax.rem(other, 2), other // 2], tot_send.at[other],
             tot_recv.at[other], (x, other))
 
-    for k in range(1, clus):
-        tot_out(k).start()
+    hooks = ((first_half,), (tile_sums,), (second_half, cluster_sums), (reduce_sums,))
+
+    def step(n, carry):
+        half, pair = n // 2, lax.rem(n, 2)
+        for number, hook in enumerate(hooks):
+            @pl.when(n == number)
+            def _():
+                for work in hook:
+                    work()
+
+        def one_head(hh, inner):
+            attend(half, pair, hh)
+            return inner
+
+        lax.fori_loop(0, 2, one_head, 0)
+
+        def one_dest(k, inner):
+            ship(half, pair * 8 + k)
+            return inner
+
+        lax.fori_loop(0, 8, one_dest, 0)
+        return carry
+
+    lax.fori_loop(0, 4, step, 0)
     for k in range(1, clus):
         tot_in(k).wait_recv()
 
@@ -356,7 +416,8 @@
     for h in range(4):
         p, hh = h // 2, h % 2
         totals = tot_rx[p].reshape(chips * 8, DH)
-        queries = q_ref[h, pl.ds(pl.multiple_of(block * 128, 128), 128), :].astype(jnp.float32)
+        taken = q_ref[pl.ds(pl.multiple_of(block * QBLK, QBLK), QBLK), h * wide : (h + 1) * wide]
+        queries = regroup(taken).astype(jnp.float32)
         approx = lax.dot_general(
             totals, queries, nt, precision=highest, preferred_element_type=jnp.float32)
         approx = approx * (log2_scale / count) + ab_ref[h]
@@ -378,7 +439,8 @@
             precision=highest, preferred_element_type=jnp.float32)
         for source in range(2 * chips):
             numer = numer + mine[:, source : source + 1] * o_rx[p, source, hh].astype(jnp.float32)
-        out_ref[h] = numer.astype(jnp.bfloat16)
+        out_ref[:, h * wide : (h + 1) * wide] = numer.reshape(32 // GROUP, GROUP, DH).reshape(
+            32 // GROUP, wide).astype(jnp.bfloat16)
 
     for copy in small + far_kv[0] + far_kv[1] + [ts_copy]:
         copy.wait_send()
@@ -391,7 +453,7 @@
         for half in range(2):
             @pl.when((dest != i) if half == 0 else (dest >= 0))
             def _():
-                _, device, parts = parts_for(half, dest // 4, lax.rem(dest, 4))
+                device, parts = parts_for(half, dest)
                 for src, dst, send_sem, recv_sem in parts:
                     remote(src, dst, send_sem, recv_sem, device).wait_send()
         return carry
@@ -409,8 +471,6 @@
     query_count = prompt_queries.shape[0]
     heads = prompt_queries.shape[1] // (GROUP * DH)
     blocks = query_count // QBLK
-    queries = prompt_queries.reshape(query_count, heads, GROUP, DH).transpose(1, 0, 2, 3)
-    queries = queries.reshape(heads, query_count * GROUP, DH)
 
     ids = tile_cluster.reshape(2, 2, 2, tiles)
     ids = jnp.where(x == 0, ids, ids[:, :, ::-1])
@@ -420,7 +480,9 @@
     live = jnp.any(
         ids[:, :, :, None, :, None] == listed_mine[:, :, None, :, None, :], axis=-1)
     tables = jnp.where(live, 0.0, dead).transpose(2, 0, 1, 3, 4).reshape(2, 2, 2 * blocks, tiles)
-    tables = jnp.pad(tables, ((0, 0), (0, 0), (0, 0), (0, 128 - tiles)))
+    shifted = [jnp.pad(tables[:, side], ((0, 0), (0, 0), (side * tiles, 128 - (1 + side) * tiles)))
+               for side in range(2)]
+    tables = jnp.stack(shifted, axis=1)
 
     r = jnp.arange(8 * chips, dtype=jnp.int32)
     number, kv_r, hh_r = 2 * (r // 8) + r % 2, (r // 4) % 2, (r // 2) % 2
@@ -445,18 +507,19 @@
     share = query_count * GROUP // clus
     vmem = pl.BlockSpec(memory_space=pltpu.VMEM)
     anywhere = pl.BlockSpec(memory_space=pl.ANY)
-    out = pl.pallas_call(
+    return pl.pallas_call(
         fast_kernel,
-        out_shape=jax.ShapeDtypeStruct((heads, share, DH), bf16),
+        out_shape=jax.ShapeDtypeStruct((query_count // clus, heads * GROUP * DH), bf16),
         in_specs=[anywhere, anywhere, vmem, vmem, vmem, vmem],
         out_specs=vmem,
         scratch_shapes=[
             pltpu.VMEM((2, 2, 2 * rows, DH), bf16),
             pltpu.VMEM((2, 2, 2 * rows, DH), bf16),
-            pltpu.VMEM((2, query_count * GROUP, DH), bf16),
+            pltpu.VMEM((query_count, 2 * GROUP * DH), bf16),
+            pltpu.VMEM((2, 2, query_count * GROUP, DH), bf16),
             pltpu.VMEM((3, 2 * blocks, 128), f32),
             pltpu.VMEM((8 * chips, 16 * tiles), f32),
-            pltpu.VMEM((2, 2 * blocks, 2 * rows), f32),
+            pltpu.VMEM((2, 2 * blocks, 128), f32),
             pltpu.VMEM((2, clus, 2, share, DH), bf16),
             pltpu.VMEM((2, blocks, 8, 128), f32),
             pltpu.VMEM((2, clus, 2, share, DH), bf16),
@@ -468,6 +531,7 @@
             pltpu.VMEM((8, DH), f32),
             pltpu.VMEM((2, chips, 8, DH), f32),
             pltpu.VMEM((128, 128), f32),
+            pltpu.VMEM((2 * rows, 128), bf16),
             dma((8,)), dma((8,)), dma((8,)), dma((5,)), dma((5,)),
             dma((2, clus)), dma((2, clus)), dma((2, clus)), dma((2, clus)),
             dma((2,)), dma((chips,)), dma((chips,)), dma((clus,)), dma((clus,)),
@@ -476,10 +540,8 @@
             collective_id=0, has_side_effects=True, vmem_limit_bytes=48 * 1024 * 1024),
     )(
         key_cache.reshape(rows, width), value_cache.reshape(rows, width),
-        queries, tables, member, approx_bias,
-    )
-    out = out.reshape(heads, query_count // clus, GROUP, DH).transpose(1, 0, 2, 3)
-    return out.reshape(query_count // clus, heads * GROUP * DH)
+        prompt_queries, tables, member, approx_bias,
+    )
 
 
 def solution(mesh):

time: 42.4 us -> 47.7 us (1.12)
  the two profiles are of different devices: /device:TPU:0 before, /device:TPU:25 now
where the time goes in v2:
time: 47.7 us; the launch traced here: 47.4 us
  Pallas kernels  38.7 us (81%)
  local copies, waits for them, and re-layouts  6.61 us (14%)
  other arithmetic  1.99 us (4%)
    pallas_call x1, Pallas kernels, fast_local(): pl.pallas_call(fast_kernel, out_shape=jax.ShapeDtypeStruct((query_count /...  38.7 us
    unnamed x7, local copies, waits for them, and re-layouts  4.84 us

profile of v2, /device:TPU:25, one launch (start us, length us, event | category | flops | bytes accessed | tf_op | source)
XLA Modules:
  0.0 47.4 jit_solution(8963116451572197388)
XLA Ops:
  0.1 0.7 %constant_dynamic-slice_fusion = s32[4,1,4]{2,1,0:T(1,128)S(1)} fusion(s32[4,4,4]{2,1,0:T(4,128)} %param.9, s32[]{:T(128)S(6)} %select_n.204), kind=kLoop, calls=%fused_computation.57 | loop fusion | bytes 132 | tf_op jit(solution)/shard_map/jit(dynamic_index_in_dim)/dynamic_slice | solution.py:498
  0.8 0.1 compare_reduce_fusion.1
  0.9 0.1 and_select_fusion
  0.9 0.7 %rev.9 = s32[2,2,2,8]{3,2,1,0:T(2,128)S(1)} reverse(s32[2,2,2,8]{3,2,1,0:T(2,128)} %bitcast.19), dimensions={2} | reverse | bytes 512 | tf_op jit(solution)/shard_map/rev | solution.py:476
  1.7 0.7 %broadcast_select_fusion = s32[2,2,2,8]{3,2,1,0:T(2,128)S(1)} fusion(s32[2,2,2,8]{3,2,1,0:T(2,128)} %bitcast.20, s32[2,2,2,8]{3,2,1,0:T(2,128)S(1)} %rev.9, pred[]{:T(512)S(6)} %eq.137), kind=kLoop, calls=%fused_computation.12 | loop fusion | flops 64 | bytes 769 | tf_op jit(solution)/shard_map/jit(_where)/select_n | solution.py:476
  2.4 0.1 broadcast_in_dim.22
  2.5 0.1 eq.141
  2.5 0.1 compare_and_fusion
  2.6 0.8 %reverse_select_fusion = s32[2,2,4,4]{3,2,1,0:T(4,128)S(1)} fusion(s32[2,2,4,4]{3,2,1,0:T(4,128)} %bitcast.21, pred[]{:T(512)S(6)} %eq.136), kind=kLoop, calls=%fused_computation.5 | loop fusion | flops 64 | bytes 513 | tf_op jit(solution)/shard_map/jit(_where)/select_n | solution.py:479
  3.4 0.1 compare_reduce_fusion
  3.6 0.1 pad_bitcast_fusion
  3.7 0.1 and_convert_fusion.a_ref
  3.8 0.1 broadcast_in_dim.28.ab_ref
  3.9 0.0 copy-start
  3.9 1.6 %copy-done = bf16[1,1024,1024]{2,1,0:T(8,128)(2,1)S(1)} copy-done((bf16[1,1024,1024]{2,1,0:T(8,128)(2,1)S(1)}, bf16[1,1024,1024]{2,1,0:T(8,128)(2,1)}, u32[]{:S(2)}) %copy-start) | copy-done | bytes 2097176
  5.4 0.0 copy-start.1
  5.5 1.6 %copy-done.1 = bf16[1,1024,1024]{2,1,0:T(8,128)(2,1)S(1)} copy-done((bf16[1,1024,1024]{2,1,0:T(8,128)(2,1)S(1)}, bf16[1,1024,1024]{2,1,0:T(8,128)(2,1)}, u32[]{:S(2)}) %copy-start.1) | copy-done | bytes 2097176
  7.0 0.0 copy-start.2
  7.0 1.0 %copy-done.2 = bf16[64,4096]{1,0:T(8,128)(2,1)S(1)} copy-done((bf16[64,4096]{1,0:T(8,128)(2,1)S(1)}, bf16[64,4096]{1,0:T(8,128)(2,1)}, u32[]{:S(2)}) %copy-start.2) | copy-done | bytes 524312
  8.1 38.7 %shard_map.55 = bf16[4,4096]{1,0:T(4,128)(2,1)S(1)} custom-call(bf16[1024,1024]{1,0:T(8,128)(2,1)S(1)} %bitcast.16, bf16[1024,1024]{1,0:T(8,128)(2,1)S(1)} %bitcast.17, bf16[64,4096]{1,0:T(8,128)(2,1)S(1)} %copy-done.2, f32[2,2,8,128]{3,2,1,0:T(8,128)S(1)} %pad_maximum_fusion.bt_ref, f32[2,64,128]{2,1,0:T(8,128)S(1)} %and_convert_fusion.a_ref, ...), custom_call_target="tpu_custom_call" | custom-call | tf_op jit(solution)/shard_map/pallas_call | solution.py:510
  46.8 0.6 %copy.8 = bf16[4,4096]{1,0:T(4,128)(2,1)} copy(bf16[4,4096]{1,0:T(4,128)(2,1)S(1)} %shard_map.55) | data formatting | bytes 65536
  (13 shorter events, 0.1 us)
Async XLA Ops:
  3.9 1.6 %copy-start = (bf16[1,1024,1024]{2,1,0:T(8,128)(2,1)S(1)}, bf16[1,1024,1024]{2,1,0:T(8,128)(2,1)}, u32[]{:S(2)}) copy-start(bf16[1,1024,1024]{2,1,0:T(8,128)(2,1)} %param.5) | copy-start | bytes 6291460
  5.4 1.6 %copy-start.1 = (bf16[1,1024,1024]{2,1,0:T(8,128)(2,1)S(1)}, bf16[1,1024,1024]{2,1,0:T(8,128)(2,1)}, u32[]{:S(2)}) copy-start(bf16[1,1024,1024]{2,1,0:T(8,128)(2,1)} %param.6) | copy-start | bytes 6291460
  7.0 1.0 %copy-start.2 = (bf16[64,4096]{1,0:T(8,128)(2,1)S(1)}, bf16[64,4096]{1,0:T(8,128)(2,1)}, u32[]{:S(2)}) copy-start(bf16[64,4096]{1,0:T(8,128)(2,1)} %q_ref.1) | copy-start | bytes 1572868

commit v3 on v2

--- a/solution.py
+++ b/solution.py
@@ -149,8 +149,8 @@
 
 
 def fast_kernel(
-    k_hbm, v_hbm, q_ref, bt_ref, a_ref, ab_ref, out_ref,
-    kbuf, vbuf, qx, qall, btx, ax, bias, o_buf, st_buf, o_rx, st_rx,
+    k_hbm, v_hbm, q_ref, ids_ref, listed_ref, out_ref,
+    kbuf, vbuf, kout, vout, qx, qall, bt, btx, bias, o_buf, st_buf, o_rx, st_rx,
     ts_buf, ts_rx, cs_buf, cs_rx, red_buf, tot_rx, wt, hot_ref,
     loc_sem, kv_send, kv_recv, in_send, in_recv,
     o_send, o_recv, st_send, st_recv, ts_sem, cs_send, cs_recv, tot_send, tot_recv,
@@ -167,25 +167,30 @@
     me = x * clus + i
     wide = GROUP * DH
     span = 2 * QBLK * GROUP
+    far = jnp.where(i < chips, 1, 0)
+    listing = listed_ref.shape[2]
 
     def pair_of(half, core):
         return 2 * (x if half == 0 else 1 - x) + core
 
-    def kv_copies(half, remote):
+    def kv_copies(half, kind):
         copies = []
         for hh in range(2):
-            for n, (src, dst) in enumerate(((k_hbm, kbuf), (v_hbm, vbuf))):
+            for n, (src, dst, out) in enumerate(((k_hbm, kbuf, kout), (v_hbm, vbuf, vout))):
                 number = half * 4 + hh * 2 + n
-                pair = pair_of(half, 1 - c if remote else c)
+                pair = pair_of(half, c if kind == 0 else 1 - c)
                 column = pl.ds(pl.multiple_of((pair * 2 + hh) * DH, DH), DH)
-                if remote:
+                if kind == 0:
+                    copies.append(pltpu.make_async_copy(
+                        src.at[:, column], dst.at[half, hh, pl.ds(0, rows)], loc_sem.at[0, number]))
+                elif kind == 1:
+                    copies.append(pltpu.make_async_copy(
+                        src.at[:, column], out.at[half, hh], loc_sem.at[1, number]))
+                else:
                     copies.append(pltpu.make_async_remote_copy(
-                        src_ref=src.at[:, column], dst_ref=dst.at[half, hh, pl.ds(rows, rows)],
+                        src_ref=out.at[half, hh], dst_ref=dst.at[half, hh, pl.ds(rows, rows)],
                         send_sem=kv_send.at[number], recv_sem=kv_recv.at[number],
                         device_id=(x, sib), device_id_type=MESH))
-                else:
-                    copies.append(pltpu.make_async_copy(
-                        src.at[:, column], dst.at[half, hh, pl.ds(0, rows)], loc_sem.at[number]))
         return copies
 
     def remote(src, dst, send_sem, recv_sem, device):
@@ -193,9 +198,10 @@
             src_ref=src, dst_ref=dst, send_sem=send_sem, recv_sem=recv_sem,
             device_id=device, device_id_type=MESH)
 
-    own_kv = [kv_copies(0, False), kv_copies(1, False)]
-    far_kv = [kv_copies(0, True), kv_copies(1, True)]
-    for copy in own_kv[0] + own_kv[1]:
+    own_kv = [kv_copies(0, 0), kv_copies(1, 0)]
+    out_kv = [kv_copies(0, 1), kv_copies(1, 1)]
+    far_kv = [kv_copies(0, 2), kv_copies(1, 2)]
+    for copy in out_kv[0] + out_kv[1] + own_kv[0] + own_kv[1]:
         copy.start()
 
     barrier = pltpu.get_barrier_semaphore()
@@ -207,23 +213,83 @@
         return carry
 
     lax.fori_loop(1, 2 * clus, greet, 0)
-    pl.semaphore_wait(barrier, 2 * clus - 1)
-
-    small = [
-        remote(bt_ref.at[0, 1], btx.at[0], in_send.at[0], in_recv.at[0], (x, sib)),
-        remote(bt_ref.at[1, 0], btx.at[1], in_send.at[1], in_recv.at[1], (1 - x, i)),
-        remote(bt_ref.at[1, 1], btx.at[2], in_send.at[2], in_recv.at[2], (1 - x, sib)),
-        remote(a_ref.at[1], ax, in_send.at[3], in_recv.at[3], (x, sib)),
-        remote(q_ref.at[:, pl.ds(pl.multiple_of(c * 2 * wide, 128), 2 * wide)], qx,
-               in_send.at[4], in_recv.at[4], (1 - x, i)),
-    ]
-    for copy in small[:3] + far_kv[0] + small[4:] + small[3:4] + far_kv[1]:
-        copy.start()
+
+    lane8 = lax.broadcasted_iota(jnp.int32, (8, 128), 1)
+    sub8 = lax.broadcasted_iota(jnp.int32, (8, 128), 0)
+    for turn in range(2):
+        pair = c if turn == 0 else 1 - c
+        named = []
+        for l in range(listing):
+            table = jnp.zeros((8, 128), jnp.int32)
+            for hh in range(2):
+                for b in range(4):
+                    table = jnp.where(sub8 == hh * 4 + b, listed_ref[2 * pair + hh, b, l], table)
+            named.append(table)
+        first = turn * tiles
+        for side in range(2):
+            slab = x if side == 0 else 1 - x
+            held = jnp.full((8, 128), -1, jnp.int32)
+            for hh in range(2):
+                for t in range(tiles):
+                    here = (lane8 == first + t) & (sub8 // 4 == hh)
+                    held = jnp.where(here, ids_ref[2 * pair + hh, 0, slab, t, 0], held)
+            live = (lane8 < first) | (lane8 >= first + tiles)
+            for table in named:
+                live = live | (held == table)
+            bt[side, turn] = jnp.where(live, 0.0, dead)
+
+    key_tile = lax.broadcasted_iota(jnp.int32, (2 * rows, 128), 0) // TILE
+    hot = key_tile == lax.broadcasted_iota(jnp.int32, (2 * rows, 128), 1)
+    hot_ref[...] = jnp.where(hot, 1.0, 0.0).astype(jnp.bfloat16)
 
     def regroup(rows_in):
         count_in = rows_in.shape[0]
         split = rows_in.astype(jnp.float32).reshape(count_in, GROUP, DH)
         return split.reshape(count_in * GROUP, DH).astype(jnp.bfloat16)
+
+    def place_queries(half, source, first):
+        def block_of(n, carry):
+            hh, block = n // 4, lax.rem(n, 4)
+            for head in range(2):
+                @pl.when(hh == head)
+                def _():
+                    columns = pl.ds(pl.multiple_of(first + head * wide, 128), wide)
+                    taken = source[pl.ds(pl.multiple_of(block * QBLK, QBLK), QBLK), columns]
+                    qall[half, head, pl.ds(pl.multiple_of(block * 128, 128), 128), :] = regroup(
+                        taken)
+            return carry
+
+        lax.fori_loop(0, 8, block_of, 0)
+
+    place_queries(0, q_ref, c * 2 * wide)
+    pl.semaphore_wait(barrier, 2 * clus - 1)
+    for copy in out_kv[0] + out_kv[1]:
+        copy.wait()
+
+    small = [
+        remote(bt.at[0, 1], btx.at[0], in_send.at[0], in_recv.at[0], (x, sib)),
+        remote(bt.at[1, 0], btx.at[1], in_send.at[1], in_recv.at[1], (1 - x, i)),
+        remote(bt.at[1, 1], btx.at[2], in_send.at[2], in_recv.at[2], (1 - x, sib)),
+        remote(q_ref.at[:, pl.ds(pl.multiple_of(c * 2 * wide, 128), 2 * wide)], qx,
+               in_send.at[3], in_recv.at[3], (1 - x, i)),
+    ]
+    for copy in small + far_kv[0] + far_kv[1]:
+        copy.start()
+
+    for copy in own_kv[0] + own_kv[1]:
+        copy.wait()
+
+    def add_up(n, carry):
+        half, hh = n // 2, lax.rem(n, 2)
+        for m, (buf, out) in enumerate(((kbuf, kout), (vbuf, vout))):
+            for part, core in ((buf[half, hh, :rows], c), (out[half, hh], 1 - c)):
+                ts_buf[half, m, 2 * core + hh] = jnp.sum(
+                    part.astype(jnp.float32).reshape(tiles, TILE, DH), axis=1)
+        return carry
+
+    lax.fori_loop(0, 4, add_up, 0)
+    ts_copy = remote(ts_buf.at[1], ts_rx, ts_sem.at[0], ts_sem.at[1], (1 - x, i))
+    ts_copy.start()
 
     def parts_for(half, dest):
         device = (x + half * (1 - 2 * x), dest)
@@ -238,11 +304,6 @@
 
     def as_row(column):
         return jnp.sum(jnp.where(square, column, 0.0), axis=0, keepdims=True)
-
-    key_tile = lax.broadcasted_iota(jnp.int32, (2 * rows, 128), 0) // TILE
-    hot = key_tile == lax.broadcasted_iota(jnp.int32, (2 * rows, 128), 1)
-    hot_ref[...] = jnp.where(hot, 1.0, 0.0).astype(jnp.bfloat16)
-    st_buf[...] = jnp.zeros_like(st_buf)
 
     def attend(half, pair, hh):
         start = pl.multiple_of(pair * span, span)
@@ -283,102 +344,84 @@
             for src, dst, send_sem, recv_sem in parts:
                 pltpu.make_async_copy(src, dst, recv_sem).start()
 
-    def place_queries(half, source, first):
-        def block_of(n, carry):
-            hh, block = n // 4, lax.rem(n, 4)
-            for head in range(2):
-                @pl.when(hh == head)
-                def _():
-                    columns = pl.ds(pl.multiple_of(first + head * wide, 128), wide)
-                    taken = source[pl.ds(pl.multiple_of(block * QBLK, QBLK), QBLK), columns]
-                    qall[half, head, pl.ds(pl.multiple_of(block * 128, 128), 128), :] = regroup(
-                        taken)
-            return carry
-
-        lax.fori_loop(0, 8, block_of, 0)
-
     def first_half():
-        for copy in own_kv[0]:
-            copy.wait()
-        place_queries(0, q_ref, c * 2 * wide)
         small[0].wait_recv()
         for copy in far_kv[0]:
             copy.wait_recv()
-        bias[0] = bt_ref[0, 0] + btx[0]
-
-    def tile_sums():
-        for copy in own_kv[1]:
-            copy.wait()
+        bias[0] = bt[0, 0] + btx[0]
+
+    def second_half():
+        for copy in small[1:]:
+            copy.wait_recv()
         for copy in far_kv[1]:
-            copy.wait_recv()
-
-        def add_up(n, carry):
-            half, hh = n // 2, lax.rem(n, 2)
-            for m, buf in enumerate((kbuf, vbuf)):
-                for side in range(2):
-                    part = buf[half, hh, side * rows : (side + 1) * rows]
-                    ts_buf[half, m, hh, side] = jnp.sum(
-                        part.astype(jnp.float32).reshape(tiles, TILE, DH), axis=1)
-            return carry
-
-        lax.fori_loop(0, 4, add_up, 0)
-        ts_copy.start()
-
-    def second_half():
-        for copy in [small[1], small[2], small[4]]:
             copy.wait_recv()
         place_queries(1, qx, 0)
         bias[1] = btx[1] + btx[2]
 
-    ts_copy = remote(ts_buf.at[1], ts_rx, ts_sem.at[0], ts_sem.at[1], (1 - x, i))
+    line = lax.broadcasted_iota(jnp.int32, (128, 128), 0)
 
     def cluster_sums():
-        small[3].wait_recv()
+        lane = lax.rem(lane8, 8 * tiles)
+        held = jnp.zeros((8, 128), jnp.int32)
+        for h in range(4):
+            for side in range(2):
+                slab = x if side == 0 else 1 - x
+                for t in range(tiles):
+                    held = jnp.where(
+                        lane == (h * 2 + side) * tiles + t, ids_ref[h, 0, slab, t, 0], held)
+        held = jnp.concatenate([held] * 16, axis=0)
+        column = lax.broadcasted_iota(jnp.int32, (128, 128), 1)
+        belongs = (held == line // 8) & (lax.rem(line, 8) == column // (2 * tiles))
         ts_copy.wait_recv()
         all_sums = jnp.concatenate(
             [ts_buf[0].reshape(8, tiles, DH), ts_rx[...].reshape(8, tiles, DH)], axis=1
         ).reshape(16 * tiles, DH)
         clustered = jnp.dot(
-            a_ref[0] + ax[...], all_sums, precision=highest, preferred_element_type=jnp.float32)
-        cs_buf[...] = clustered.reshape(chips, 8, DH)
-        cs_rx[w] = cs_buf[w]
-        for k in range(1, chips):
-            cs_out(k).start()
-
-    def cs_out(k):
-        chip = lax.rem(w + k, chips)
+            jnp.where(belongs, 1.0, 0.0), all_sums, precision=highest,
+            preferred_element_type=jnp.float32)
+        cs_buf[...] = clustered.reshape(clus, 8, DH)
+        cs_rx[i] = cs_buf[i]
+        lax.fori_loop(1, clus, start_cs, 0)
+
+    def cs_copy(k, out):
+        other = lax.rem(i + k, clus)
         return remote(
-            cs_buf.at[chip], cs_rx.at[w], cs_send.at[chip], cs_recv.at[w], (x, 2 * chip + c))
-
-    def cs_in(k):
-        chip = lax.rem(w + k, chips)
+            cs_buf.at[other], cs_rx.at[i if out else other], cs_send.at[other],
+            cs_recv.at[i if out else other], (x, other))
+
+    def start_cs(k, carry):
+        cs_copy(k, True).start()
+        return carry
+
+    def tot_copy(k, out):
+        other = lax.rem(i + k, clus)
         return remote(
-            cs_buf.at[chip], cs_rx.at[chip], cs_send.at[chip], cs_recv.at[chip], (x, 2 * chip + c))
+            red_buf, tot_rx.at[i if out else other], tot_send.at[other],
+            tot_recv.at[i if out else other], (x, other))
+
+    def start_tot(k, carry):
+        tot_copy(k, True).start()
+        return carry
+
+    def wait_cs(k, carry):
+        cs_copy(k, False).wait_recv()
+        return carry
+
+    def wait_tot(k, carry):
+        tot_copy(k, False).wait_recv()
+        return carry
 
     def reduce_sums():
-        for k in range(1, chips):
-            cs_in(k).wait_recv()
+        lax.fori_loop(1, clus, wait_cs, 0)
         reduced = jnp.sum(cs_rx[...], axis=0)
         red_buf[...] = reduced
-        tot_rx[c, w] = reduced
-        for k in range(1, clus):
-            tot_out(k).start()
-
-    def tot_out(k):
-        other = lax.rem(i + k, clus)
-        return remote(
-            red_buf, tot_rx.at[c, w], tot_send.at[other], tot_recv.at[i], (x, other))
-
-    def tot_in(k):
-        other = lax.rem(i + k, clus)
-        return remote(
-            red_buf, tot_rx.at[lax.rem(other, 2), other // 2], tot_send.at[other],
-            tot_recv.at[other], (x, other))
-
-    hooks = ((first_half,), (tile_sums,), (second_half, cluster_sums), (reduce_sums,))
+        tot_rx[i] = reduced
+        lax.fori_loop(1, clus, start_tot, 0)
+
+    hooks = ((first_half,), (cluster_sums,), (reduce_sums, second_half))
 
     def step(n, carry):
-        half, pair = n // 2, lax.rem(n, 2)
+        half, pair = n // 2, lax.rem(n + far, 2)
         for number, hook in enumerate(hooks):
             @pl.when(n == number)
             def _():
@@ -392,15 +435,34 @@
         lax.fori_loop(0, 2, one_head, 0)
 
         def one_dest(k, inner):
-            ship(half, pair * 8 + k)
+            ship(half, pair * 8 + lax.rem(k + i, 8))
             return inner
 
         lax.fori_loop(0, 8, one_dest, 0)
         return carry
 
     lax.fori_loop(0, 4, step, 0)
-    for k in range(1, clus):
-        tot_in(k).wait_recv()
+    lax.fori_loop(1, clus, wait_tot, 0)
+    block, part = i // 4, lax.rem(i, 4)
+    share = pl.ds(pl.multiple_of(part * 32, 32), 32)
+    totals = tot_rx[...].reshape(clus * 8, DH)
+    approx_parts = []
+    for h in range(4):
+        taken = q_ref[pl.ds(pl.multiple_of(block * QBLK, QBLK), QBLK), h * wide : (h + 1) * wide]
+        queries = regroup(taken).astype(jnp.float32)
+        approx = lax.dot_general(
+            totals, queries, nt, precision=highest, preferred_element_type=jnp.float32)
+        usable = lax.rem(line, 8) == h
+        for l in range(listing):
+            usable = usable & (line // 8 != listed_ref[h, block, l])
+        approx = jnp.where(usable, approx * (log2_scale / count), dead)
+        top = jnp.max(approx, axis=0, keepdims=True)
+        approx_weight = jnp.where(usable, jnp.exp2(approx - top), 0.0)
+        total = count * jnp.sum(approx_weight, axis=0, keepdims=True)
+        wt[h] = pltpu.roll(approx_weight, 4, 0).T
+        numer = jnp.dot(
+            wt[h, share, :], totals, precision=highest, preferred_element_type=jnp.float32)
+        approx_parts.append((top, total, numer))
 
     def arrive(n, carry):
         core, source = n // clus, lax.rem(n, clus)
@@ -412,31 +474,23 @@
 
     lax.fori_loop(0, 2 * clus, arrive, 0)
 
-    block, part = i // 4, lax.rem(i, 4)
     for h in range(4):
         p, hh = h // 2, h % 2
-        totals = tot_rx[p].reshape(chips * 8, DH)
-        taken = q_ref[pl.ds(pl.multiple_of(block * QBLK, QBLK), QBLK), h * wide : (h + 1) * wide]
-        queries = regroup(taken).astype(jnp.float32)
-        approx = lax.dot_general(
-            totals, queries, nt, precision=highest, preferred_element_type=jnp.float32)
-        approx = approx * (log2_scale / count) + ab_ref[h]
         tops, sums = st_rx[p, :, 2 * hh, :], st_rx[p, :, 2 * hh + 1, :]
-        top = jnp.maximum(
-            jnp.max(tops, axis=0, keepdims=True), jnp.max(approx, axis=0, keepdims=True))
+        approx_top, approx_total, _ = approx_parts[h]
+        top = jnp.maximum(jnp.max(tops, axis=0, keepdims=True), approx_top)
         factor = jnp.exp2(tops - top)
-        approx_weight = jnp.exp2(approx - top)
-        total = jnp.sum(factor * sums, axis=0, keepdims=True) + count * jnp.sum(
-            approx_weight, axis=0, keepdims=True)
+        approx_factor = jnp.exp2(approx_top - top)
+        total = jnp.sum(factor * sums, axis=0, keepdims=True) + approx_factor * approx_total
         inverse = 1.0 / total
         mixed = jnp.concatenate(
-            [factor * inverse, jnp.zeros((48, 128), jnp.float32),
-             pltpu.roll(approx_weight * inverse, 4, 0)], axis=0)
-        wt[...] = mixed.T
-        mine = wt[pl.ds(pl.multiple_of(part * 32, 32), 32), :]
-        numer = jnp.dot(
-            mine, jnp.concatenate([jnp.zeros((64, DH), jnp.float32), totals], axis=0),
-            precision=highest, preferred_element_type=jnp.float32)
+            [factor * inverse, jnp.broadcast_to(approx_factor * inverse, (8, 128)),
+             jnp.zeros((104, 128), jnp.float32)], axis=0)
+        wt[4 + h] = mixed.T
+    for h in range(4):
+        p, hh = h // 2, h % 2
+        mine = wt[4 + h, share, :]
+        numer = mine[:, 2 * chips : 2 * chips + 1] * approx_parts[h][2]
         for source in range(2 * chips):
             numer = numer + mine[:, source : source + 1] * o_rx[p, source, hh].astype(jnp.float32)
         out_ref[:, h * wide : (h + 1) * wide] = numer.reshape(32 // GROUP, GROUP, DH).reshape(
@@ -444,10 +498,13 @@
 
     for copy in small + far_kv[0] + far_kv[1] + [ts_copy]:
         copy.wait_send()
-    for k in range(1, chips):
-        cs_out(k).wait_send()
-    for k in range(1, clus):
-        tot_out(k).wait_send()
+
+    def drain(k, carry):
+        cs_copy(k, True).wait_send()
+        tot_copy(k, True).wait_send()
+        return carry
+
+    lax.fori_loop(1, clus, drain, 0)
 
     def sent(dest, carry):
         for half in range(2):
@@ -463,84 +520,53 @@
 
 def fast_local(key_cache, value_cache, prompt_queries, tile_cluster, listed_clusters):
     clus = lax.axis_size("clus")
-    x, i = lax.axis_index("head"), lax.axis_index("clus")
-    c = lax.rem(i, 2)
     _, rows, width = key_cache.shape
     tiles = rows // TILE
-    chips = clus // 2
     query_count = prompt_queries.shape[0]
     heads = prompt_queries.shape[1] // (GROUP * DH)
     blocks = query_count // QBLK
-
-    ids = tile_cluster.reshape(2, 2, 2, tiles)
-    ids = jnp.where(x == 0, ids, ids[:, :, ::-1])
-    ids = jnp.where(c == 0, ids, ids[::-1])
-    listed = listed_clusters.reshape(2, 2, blocks, -1)
-    listed_mine = jnp.where(c == 0, listed, listed[::-1])
-    live = jnp.any(
-        ids[:, :, :, None, :, None] == listed_mine[:, :, None, :, None, :], axis=-1)
-    tables = jnp.where(live, 0.0, dead).transpose(2, 0, 1, 3, 4).reshape(2, 2, 2 * blocks, tiles)
-    shifted = [jnp.pad(tables[:, side], ((0, 0), (0, 0), (side * tiles, 128 - (1 + side) * tiles)))
-               for side in range(2)]
-    tables = jnp.stack(shifted, axis=1)
-
-    r = jnp.arange(8 * chips, dtype=jnp.int32)
-    number, kv_r, hh_r = 2 * (r // 8) + r % 2, (r // 4) % 2, (r // 2) % 2
-    k = jnp.arange(16 * tiles, dtype=jnp.int32)
-    kv_k, hh_k, side_k = k // (8 * tiles), (k // (4 * tiles)) % 2, (k // (2 * tiles)) % 2
-    same = (kv_r[:, None] == kv_k[None, :]) & (hh_r[:, None] == hh_k[None, :])
-    named = jnp.broadcast_to(
-        ids.reshape(2, 1, 2, 1, 2 * tiles), (2, 2, 2, 2, 2 * tiles)).reshape(2, 1, 16 * tiles)
-    side = jnp.arange(2, dtype=jnp.int32)[:, None, None]
-    member = (named == number[None, :, None]) & same[None] & (side_k[None, None, :] == side)
-    member = member.astype(jnp.float32)
-
-    listed_here = lax.dynamic_index_in_dim(
-        listed_clusters, i * blocks // clus, 1, keepdims=False)
-    skipped = jnp.any(listed_here[:, :, None] == number, axis=1)
-    usable = (kv_r == 0)[None] & (hh_r[None] == (jnp.arange(heads) % 2)[:, None]) & ~skipped
-    approx_bias = jnp.broadcast_to(
-        jnp.where(usable, 0.0, dead)[:, :, None], (heads, 8 * chips, 128))
-
     dma = pltpu.SemaphoreType.DMA
     f32, bf16 = jnp.float32, jnp.bfloat16
     share = query_count * GROUP // clus
     vmem = pl.BlockSpec(memory_space=pltpu.VMEM)
-    anywhere = pl.BlockSpec(memory_space=pl.ANY)
+    smem = pl.BlockSpec(memory_space=pltpu.SMEM)
+    hbm = pl.BlockSpec(memory_space=pltpu.HBM)
     return pl.pallas_call(
         fast_kernel,
         out_shape=jax.ShapeDtypeStruct((query_count // clus, heads * GROUP * DH), bf16),
-        in_specs=[anywhere, anywhere, vmem, vmem, vmem, vmem],
+        in_specs=[hbm, hbm, vmem, smem, smem],
         out_specs=vmem,
         scratch_shapes=[
             pltpu.VMEM((2, 2, 2 * rows, DH), bf16),
             pltpu.VMEM((2, 2, 2 * rows, DH), bf16),
+            pltpu.VMEM((2, 2, rows, DH), bf16),
+            pltpu.VMEM((2, 2, rows, DH), bf16),
             pltpu.VMEM((query_count, 2 * GROUP * DH), bf16),
             pltpu.VMEM((2, 2, query_count * GROUP, DH), bf16),
+            pltpu.VMEM((2, 2, 2 * blocks, 128), f32),
             pltpu.VMEM((3, 2 * blocks, 128), f32),
-            pltpu.VMEM((8 * chips, 16 * tiles), f32),
             pltpu.VMEM((2, 2 * blocks, 128), f32),
             pltpu.VMEM((2, clus, 2, share, DH), bf16),
-            pltpu.VMEM((2, blocks, 8, 128), f32),
+            pltpu.VMEM((2, blocks, 4, 128), f32),
             pltpu.VMEM((2, clus, 2, share, DH), bf16),
-            pltpu.VMEM((2, clus, 8, 128), f32),
-            pltpu.VMEM((2, 2, 2, 2, tiles, DH), f32),
-            pltpu.VMEM((2, 2, 2, tiles, DH), f32),
-            pltpu.VMEM((chips, 8, DH), f32),
-            pltpu.VMEM((chips, 8, DH), f32),
+            pltpu.VMEM((2, clus, 4, 128), f32),
+            pltpu.VMEM((2, 2, heads, tiles, DH), f32),
+            pltpu.VMEM((2, heads, tiles, DH), f32),
+            pltpu.VMEM((clus, 8, DH), f32),
+            pltpu.VMEM((clus, 8, DH), f32),
             pltpu.VMEM((8, DH), f32),
-            pltpu.VMEM((2, chips, 8, DH), f32),
-            pltpu.VMEM((128, 128), f32),
+            pltpu.VMEM((clus, 8, DH), f32),
+            pltpu.VMEM((8, 128, 128), f32),
             pltpu.VMEM((2 * rows, 128), bf16),
-            dma((8,)), dma((8,)), dma((8,)), dma((5,)), dma((5,)),
+            dma((2, 8)), dma((8,)), dma((8,)), dma((4,)), dma((4,)),
             dma((2, clus)), dma((2, clus)), dma((2, clus)), dma((2, clus)),
-            dma((2,)), dma((chips,)), dma((chips,)), dma((clus,)), dma((clus,)),
+            dma((2,)), dma((clus,)), dma((clus,)), dma((clus,)), dma((clus,)),
         ],
         compiler_params=pltpu.CompilerParams(
-            collective_id=0, has_side_effects=True, vmem_limit_bytes=48 * 1024 * 1024),
+            collective_id=0, has_side_effects=True, vmem_limit_bytes=56 * 1024 * 1024),
     )(
         key_cache.reshape(rows, width), value_cache.reshape(rows, width),
-        prompt_queries, tables, member, approx_bias,
+        prompt_queries, tile_cluster, listed_clusters,
     )
 
 

time: 47.7 us -> 44.6 us (0.935)
  the two profiles are of different devices: /device:TPU:25 before, /device:TPU:0 now
where the time goes in v3:
time: 44.6 us; the launch traced here: 44.3 us
  Pallas kernels  41.5 us (93%)
  local copies, waits for them, and re-layouts  2.8 us (6%)
    pallas_call x1, Pallas kernels, fast_local(): pl.pallas_call(fast_kernel, out_shape=jax.ShapeDtypeStruct((query_count /...  41.5 us
    unnamed x2, local copies, waits for them, and re-layouts  2.8 us

profile of v3, /device:TPU:0, one launch (start us, length us, event | category | flops | bytes accessed | tf_op | source)
XLA Modules:
  0.0 44.3 jit_solution(12351559974265567735)
XLA Ops:
  0.0 1.4 %copy.6.ids_ref = s32[4,1,2,8,1]{4,3,2,1,0:T(8,128)} copy(s32[4,1,2,8,1]{3,4,2,1,0:T(1,128)} %param.8) | data formatting | bytes 512 | tf_op args[3]
  1.4 41.5 %shard_map.55 = bf16[4,4096]{1,0:T(4,128)(2,1)} custom-call(bf16[1024,1024]{1,0:T(8,128)(2,1)} %bitcast.2, bf16[1024,1024]{1,0:T(8,128)(2,1)} %bitcast.3, bf16[64,4096]{1,0:T(8,128)(2,1)} %q_ref.1, s32[4,1,2,8,1]{4,3,2,1,0:T(8,128)} %copy.6.ids_ref, s32[4,4,4]{2,1,0:T(4,128)} %listed_ref.1), custom_call_target="tpu_custom_call" | custom-call | tf_op jit(solution)/shard_map/pallas_call | solution.py:534
  42.9 1.4 %copy.8 = bf16[4,4096]{1,0:T(4,128)(2,1)} copy(bf16[4,4096]{1,0:T(4,128)(2,1)} %shard_map.55) | data formatting | bytes 65536

commit v4 on v3

--- a/solution.py
+++ b/solution.py
@@ -150,10 +150,10 @@
 
 def fast_kernel(
     k_hbm, v_hbm, q_ref, ids_ref, listed_ref, out_ref,
-    kbuf, vbuf, kout, vout, qx, qall, bt, btx, bias, o_buf, st_buf, o_rx, st_rx,
+    kbuf, vbuf, kout, vout, kturn, qx, qall, bt, btx, bias, o_buf, o_rx,
     ts_buf, ts_rx, cs_buf, cs_rx, red_buf, tot_rx, wt, hot_ref,
     loc_sem, kv_send, kv_recv, in_send, in_recv,
-    o_send, o_recv, st_send, st_recv, ts_sem, cs_send, cs_recv, tot_send, tot_recv,
+    o_send, o_recv, ts_sem, cs_send, cs_recv, tot_send, tot_recv,
 ):
     x, i = lax.axis_index("head"), lax.axis_index("clus")
     clus = lax.axis_size("clus")
@@ -164,7 +164,6 @@
     rows = k_hbm.shape[0]
     tiles = rows // TILE
     count = float(clus * TILE)
-    me = x * clus + i
     wide = GROUP * DH
     span = 2 * QBLK * GROUP
     far = jnp.where(i < chips, 1, 0)
@@ -206,13 +205,16 @@
 
     barrier = pltpu.get_barrier_semaphore()
 
-    def greet(k, carry):
-        other = lax.rem(me + k, 2 * clus)
-        pl.semaphore_signal(
-            barrier, inc=1, device_id=(other // clus, lax.rem(other, clus)), device_id_type=MESH)
-        return carry
-
-    lax.fori_loop(1, 2 * clus, greet, 0)
+    def ahead(k):
+        return jnp.where(i + k >= clus, i + k - clus, i + k)
+
+    def greet(side, k):
+        pl.semaphore_signal(barrier, inc=1, device_id=(side, ahead(k)), device_id_type=MESH)
+
+    for k in range(clus):
+        greet(1 - x, k)
+        if k > 0:
+            greet(x, k)
 
     lane8 = lax.broadcasted_iota(jnp.int32, (8, 128), 1)
     sub8 = lax.broadcasted_iota(jnp.int32, (8, 128), 0)
@@ -232,15 +234,27 @@
             for hh in range(2):
                 for t in range(tiles):
                     here = (lane8 == first + t) & (sub8 // 4 == hh)
-                    held = jnp.where(here, ids_ref[2 * pair + hh, 0, slab, t, 0], held)
+                    held = jnp.where(here, ids_ref[2 * (2 * pair + hh) + slab, t], held)
             live = (lane8 < first) | (lane8 >= first + tiles)
             for table in named:
                 live = live | (held == table)
             bt[side, turn] = jnp.where(live, 0.0, dead)
 
-    key_tile = lax.broadcasted_iota(jnp.int32, (2 * rows, 128), 0) // TILE
-    hot = key_tile == lax.broadcasted_iota(jnp.int32, (2 * rows, 128), 1)
+    key_tile = lax.broadcasted_iota(jnp.int32, (128, 2 * rows), 1) // TILE
+    hot = key_tile == lax.broadcasted_iota(jnp.int32, (128, 2 * rows), 0)
     hot_ref[...] = jnp.where(hot, 1.0, 0.0).astype(jnp.bfloat16)
+
+    def turn_keys(half, side):
+        def turn(n, carry):
+            hh, first = n // 2, pl.multiple_of(side * rows + lax.rem(n, 2) * (rows // 2), 128)
+            for head in range(2):
+                @pl.when(hh == head)
+                def _():
+                    part = kbuf[half, head, pl.ds(first, rows // 2), :]
+                    kturn[half, head, :, pl.ds(first, rows // 2)] = part.T
+            return carry
+
+        lax.fori_loop(0, 4, turn, 0)
 
     def regroup(rows_in):
         count_in = rows_in.shape[0]
@@ -288,24 +302,19 @@
         return carry
 
     lax.fori_loop(0, 4, add_up, 0)
+    turn_keys(0, 0)
     ts_copy = remote(ts_buf.at[1], ts_rx, ts_sem.at[0], ts_sem.at[1], (1 - x, i))
     ts_copy.start()
 
-    def parts_for(half, dest):
-        device = (x + half * (1 - 2 * x), dest)
-        return device, (
-            (o_buf.at[half, dest], o_rx.at[c, slot], o_send.at[half, dest], o_recv.at[c, slot]),
-            (st_buf.at[half, dest // 4], st_rx.at[c, slot], st_send.at[half, dest],
-             st_recv.at[c, slot]),
-        )
-
     square = lax.broadcasted_iota(jnp.int32, (128, 128), 0) == lax.broadcasted_iota(
         jnp.int32, (128, 128), 1)
 
     def as_row(column):
         return jnp.sum(jnp.where(square, column, 0.0), axis=0, keepdims=True)
 
-    def attend(half, pair, hh):
+    sub16 = lax.broadcasted_iota(jnp.int32, (16, 128), 0)
+
+    def attend(half, pair, hh, stats):
         start = pl.multiple_of(pair * span, span)
         masks = [
             jnp.broadcast_to(bias[half, pl.ds(hh * 4 + pair * 2 + n, 1), :], (128, 128))
@@ -313,41 +322,47 @@
         ]
         masks = jnp.concatenate(masks, axis=0).astype(jnp.bfloat16)
         queries = jnp.concatenate([qall[half, hh, pl.ds(start, span), :], masks], axis=1)
-        keys = jnp.concatenate([kbuf[half, hh], hot_ref[...]], axis=1)
-        scores = lax.dot_general(queries, keys, nt, preferred_element_type=jnp.float32)
+        keys = jnp.concatenate([kturn[half, hh], hot_ref[...]], axis=0)
+        scores = jnp.dot(queries, keys, preferred_element_type=jnp.float32)
         top = jnp.maximum(jnp.max(scores, axis=1, keepdims=True), lowest_top) * log2_scale
+        top = top.astype(jnp.bfloat16).astype(jnp.float32)
         weights = jnp.exp2(scores * log2_scale - top).astype(jnp.bfloat16)
         values = jnp.concatenate(
             [vbuf[half, hh], jnp.ones((2 * rows, 128), jnp.bfloat16)], axis=1)
         numer = jnp.dot(weights, values, preferred_element_type=jnp.float32)
+        after = []
         for n in range(2):
-            block = pair * 2 + n
             part = slice(128 * n, 128 * (n + 1))
-            st_buf[half, block, pl.ds(hh * 2, 1), :] = as_row(top[part])
-            st_buf[half, block, pl.ds(hh * 2 + 1, 1), :] = as_row(numer[part, DH:])
+            total = as_row(numer[part, DH:])
+            upper = total.astype(jnp.bfloat16).astype(jnp.float32)
+            held = stats[n]
+            for r, row in enumerate((as_row(top[part]), upper, total - upper)):
+                held = jnp.where(sub16 == hh * 3 + r, row, held)
+            after.append(held)
             for j in range(4):
                 first = 128 * n + 32 * j
-                o_buf[half, block * 4 + j, hh] = numer[first : first + 32, :DH].astype(
-                    jnp.bfloat16)
+                place = pl.ds(pl.multiple_of(hh * 32, 32), 32)
+                o_buf[half * clus + pair * 8 + n * 4 + j, place, :] = numer[
+                    first : first + 32, :DH].astype(jnp.bfloat16)
+        return tuple(after)
 
     def ship(half, dest):
-        device, parts = parts_for(half, dest)
+        src = o_buf.at[half * clus + dest]
         here = (half == 0) & (dest == i)
 
         @pl.when(jnp.logical_not(here))
         def _():
-            for src, dst, send_sem, recv_sem in parts:
-                remote(src, dst, send_sem, recv_sem, device).start()
+            remote(src, o_rx.at[c, slot], o_send, o_recv, (x + half * (1 - 2 * x), dest)).start()
 
         @pl.when(here)
         def _():
-            for src, dst, send_sem, recv_sem in parts:
-                pltpu.make_async_copy(src, dst, recv_sem).start()
+            pltpu.make_async_copy(src, o_rx.at[c, slot], o_recv).start()
 
     def first_half():
         small[0].wait_recv()
         for copy in far_kv[0]:
             copy.wait_recv()
+        turn_keys(0, 1)
         bias[0] = bt[0, 0] + btx[0]
 
     def second_half():
@@ -356,6 +371,8 @@
         for copy in far_kv[1]:
             copy.wait_recv()
         place_queries(1, qx, 0)
+        turn_keys(1, 0)
+        turn_keys(1, 1)
         bias[1] = btx[1] + btx[2]
 
     line = lax.broadcasted_iota(jnp.int32, (128, 128), 0)
@@ -368,7 +385,7 @@
                 slab = x if side == 0 else 1 - x
                 for t in range(tiles):
                     held = jnp.where(
-                        lane == (h * 2 + side) * tiles + t, ids_ref[h, 0, slab, t, 0], held)
+                        lane == (h * 2 + side) * tiles + t, ids_ref[2 * h + slab, t], held)
         held = jnp.concatenate([held] * 16, axis=0)
         column = lax.broadcasted_iota(jnp.int32, (128, 128), 1)
         belongs = (held == line // 8) & (lax.rem(line, 8) == column // (2 * tiles))
@@ -383,36 +400,27 @@
         cs_rx[i] = cs_buf[i]
         lax.fori_loop(1, clus, start_cs, 0)
 
-    def cs_copy(k, out):
+    def cs_copy(k):
         other = lax.rem(i + k, clus)
-        return remote(
-            cs_buf.at[other], cs_rx.at[i if out else other], cs_send.at[other],
-            cs_recv.at[i if out else other], (x, other))
+        return remote(cs_buf.at[other], cs_rx.at[i], cs_send, cs_recv, (x, other))
 
     def start_cs(k, carry):
-        cs_copy(k, True).start()
+        cs_copy(k).start()
         return carry
 
-    def tot_copy(k, out):
-        other = lax.rem(i + k, clus)
-        return remote(
-            red_buf, tot_rx.at[i if out else other], tot_send.at[other],
-            tot_recv.at[i if out else other], (x, other))
+    def tot_copy(k):
+        return remote(red_buf, tot_rx.at[i], tot_send, tot_recv, (x, lax.rem(i + k, clus)))
 
     def start_tot(k, carry):
-        tot_copy(k, True).start()
+        tot_copy(k).start()
         return carry
 
-    def wait_cs(k, carry):
-        cs_copy(k, False).wait_recv()
-        return carry
-
-    def wait_tot(k, carry):
-        tot_copy(k, False).wait_recv()
-        return carry
+    def take_all(buf, amount, sem):
+        part = buf.at[pl.ds(0, amount)]
+        pltpu.make_async_copy(part, part, sem).wait()
 
     def reduce_sums():
-        lax.fori_loop(1, clus, wait_cs, 0)
+        take_all(cs_rx, clus - 1, cs_recv)
         reduced = jnp.sum(cs_rx[...], axis=0)
         red_buf[...] = reduced
         tot_rx[i] = reduced
@@ -428,11 +436,13 @@
                 for work in hook:
                     work()
 
-        def one_head(hh, inner):
-            attend(half, pair, hh)
-            return inner
-
-        lax.fori_loop(0, 2, one_head, 0)
+        blank = jnp.zeros((16, 128), jnp.float32)
+        stats = lax.fori_loop(
+            0, 2, lambda hh, held: attend(half, pair, hh, held), (blank, blank))
+        for n in range(2):
+            packed = stats[n].astype(jnp.bfloat16)
+            for j in range(4):
+                o_buf[half * clus + pair * 8 + n * 4 + j, 64:80, :] = packed
 
         def one_dest(k, inner):
             ship(half, pair * 8 + lax.rem(k + i, 8))
@@ -442,7 +452,7 @@
         return carry
 
     lax.fori_loop(0, 4, step, 0)
-    lax.fori_loop(1, clus, wait_tot, 0)
+    take_all(tot_rx, clus - 1, tot_recv)
     block, part = i // 4, lax.rem(i, 4)
     share = pl.ds(pl.multiple_of(part * 32, 32), 32)
     totals = tot_rx[...].reshape(clus * 8, DH)
@@ -464,19 +474,11 @@
             wt[h, share, :], totals, precision=highest, preferred_element_type=jnp.float32)
         approx_parts.append((top, total, numer))
 
-    def arrive(n, carry):
-        core, source = n // clus, lax.rem(n, clus)
-        remote(o_buf.at[0, 0], o_rx.at[core, source], o_send.at[0, 0],
-               o_recv.at[core, source], (x, sib)).wait_recv()
-        remote(st_buf.at[0, 0], st_rx.at[core, source], st_send.at[0, 0],
-               st_recv.at[core, source], (x, sib)).wait_recv()
-        return carry
-
-    lax.fori_loop(0, 2 * clus, arrive, 0)
-
+    take_all(o_rx, 2, o_recv)
     for h in range(4):
         p, hh = h // 2, h % 2
-        tops, sums = st_rx[p, :, 2 * hh, :], st_rx[p, :, 2 * hh + 1, :]
+        held = o_rx[p, :, 64:80, :].astype(jnp.float32)
+        tops, sums = held[:, 3 * hh, :], held[:, 3 * hh + 1, :] + held[:, 3 * hh + 2, :]
         approx_top, approx_total, _ = approx_parts[h]
         top = jnp.maximum(jnp.max(tops, axis=0, keepdims=True), approx_top)
         factor = jnp.exp2(tops - top)
@@ -492,30 +494,15 @@
         mine = wt[4 + h, share, :]
         numer = mine[:, 2 * chips : 2 * chips + 1] * approx_parts[h][2]
         for source in range(2 * chips):
-            numer = numer + mine[:, source : source + 1] * o_rx[p, source, hh].astype(jnp.float32)
-        out_ref[:, h * wide : (h + 1) * wide] = numer.reshape(32 // GROUP, GROUP, DH).reshape(
-            32 // GROUP, wide).astype(jnp.bfloat16)
+            numer = numer + mine[:, source : source + 1] * o_rx[p, source, 32 * hh : 32 * (hh + 1), :].astype(jnp.float32)
+        out_ref[h] = numer.astype(jnp.bfloat16)
 
     for copy in small + far_kv[0] + far_kv[1] + [ts_copy]:
         copy.wait_send()
 
-    def drain(k, carry):
-        cs_copy(k, True).wait_send()
-        tot_copy(k, True).wait_send()
-        return carry
-
-    lax.fori_loop(1, clus, drain, 0)
-
-    def sent(dest, carry):
-        for half in range(2):
-            @pl.when((dest != i) if half == 0 else (dest >= 0))
-            def _():
-                device, parts = parts_for(half, dest)
-                for src, dst, send_sem, recv_sem in parts:
-                    remote(src, dst, send_sem, recv_sem, device).wait_send()
-        return carry
-
-    lax.fori_loop(0, clus, sent, 0)
+    take_all(cs_buf, clus - 1, cs_send)
+    take_all(tot_rx, clus - 1, tot_send)
+    take_all(o_buf, 2 * clus - 1, o_send)
 
 
 def fast_local(key_cache, value_cache, prompt_queries, tile_cluster, listed_clusters):
@@ -531,9 +518,9 @@
     vmem = pl.BlockSpec(memory_space=pltpu.VMEM)
     smem = pl.BlockSpec(memory_space=pltpu.SMEM)
     hbm = pl.BlockSpec(memory_space=pltpu.HBM)
-    return pl.pallas_call(
+    out = pl.pallas_call(
         fast_kernel,
-        out_shape=jax.ShapeDtypeStruct((query_count // clus, heads * GROUP * DH), bf16),
+        out_shape=jax.ShapeDtypeStruct((heads, share, DH), bf16),
         in_specs=[hbm, hbm, vmem, smem, smem],
         out_specs=vmem,
         scratch_shapes=[
@@ -541,15 +528,14 @@
             pltpu.VMEM((2, 2, 2 * rows, DH), bf16),
             pltpu.VMEM((2, 2, rows, DH), bf16),
             pltpu.VMEM((2, 2, rows, DH), bf16),
+            pltpu.VMEM((2, 2, DH, 2 * rows), bf16),
             pltpu.VMEM((query_count, 2 * GROUP * DH), bf16),
             pltpu.VMEM((2, 2, query_count * GROUP, DH), bf16),
             pltpu.VMEM((2, 2, 2 * blocks, 128), f32),
             pltpu.VMEM((3, 2 * blocks, 128), f32),
             pltpu.VMEM((2, 2 * blocks, 128), f32),
-            pltpu.VMEM((2, clus, 2, share, DH), bf16),
-            pltpu.VMEM((2, blocks, 4, 128), f32),
-            pltpu.VMEM((2, clus, 2, share, DH), bf16),
-            pltpu.VMEM((2, clus, 4, 128), f32),
+            pltpu.VMEM((2 * clus, 2 * share + 16, DH), bf16),
+            pltpu.VMEM((2, clus, 2 * share + 16, DH), bf16),
             pltpu.VMEM((2, 2, heads, tiles, DH), f32),
             pltpu.VMEM((2, heads, tiles, DH), f32),
             pltpu.VMEM((clus, 8, DH), f32),
@@ -557,17 +543,18 @@
             pltpu.VMEM((8, DH), f32),
             pltpu.VMEM((clus, 8, DH), f32),
             pltpu.VMEM((8, 128, 128), f32),
-            pltpu.VMEM((2 * rows, 128), bf16),
+            pltpu.VMEM((128, 2 * rows), bf16),
             dma((2, 8)), dma((8,)), dma((8,)), dma((4,)), dma((4,)),
-            dma((2, clus)), dma((2, clus)), dma((2, clus)), dma((2, clus)),
-            dma((2,)), dma((clus,)), dma((clus,)), dma((clus,)), dma((clus,)),
+            dma, dma, dma((2,)), dma, dma, dma, dma,
         ],
         compiler_params=pltpu.CompilerParams(
             collective_id=0, has_side_effects=True, vmem_limit_bytes=56 * 1024 * 1024),
     )(
         key_cache.reshape(rows, width), value_cache.reshape(rows, width),
-        prompt_queries, tile_cluster, listed_clusters,
-    )
+        prompt_queries, tile_cluster.reshape(2 * heads, tiles), listed_clusters,
+    )
+    out = out.reshape(heads, query_count // clus, GROUP, DH).transpose(1, 0, 2, 3)
+    return out.reshape(query_count // clus, heads * GROUP * DH)
 
 
 def solution(mesh):

time: 44.6 us -> 42.3 us (0.948)
  local copies, waits for them, and re-layouts: 2.8 us -> 1.4 us
  Pallas kernels: 41.5 us -> 40.7 us
    unnamed x2, local copies, waits for them, and re-layouts: 2.8 us -> 1.4 us
    pallas_call x1, Pallas kernels: 41.5 us -> 40.7 us  [fast_local(): pl.pallas_call(fast_kernel, out_shape=jax.ShapeDtypeStruct((heads, share,...]
where the time goes in v4:
time: 42.3 us; the launch traced here: 42.1 us
  Pallas kernels  40.7 us (96%)
  local copies, waits for them, and re-layouts  1.4 us (3%)
    pallas_call x1, Pallas kernels, fast_local(): pl.pallas_call(fast_kernel, out_shape=jax.ShapeDtypeStruct((heads, share,...  40.7 us
    unnamed x2, local copies, waits for them, and re-layouts  1.4 us

profile of v4, /device:TPU:0, one launch (start us, length us, event | category | flops | bytes accessed | tf_op | source)
XLA Modules:
  0.0 42.1 jit_solution(941277509356737862)
XLA Ops:
  0.0 40.7 %shard_map.55 = bf16[4,32,128]{2,1,0:T(8,128)(2,1)} custom-call(bf16[1024,1024]{1,0:T(8,128)(2,1)} %bitcast.14, bf16[1024,1024]{1,0:T(8,128)(2,1)} %bitcast.15, bf16[64,4096]{1,0:T(8,128)(2,1)} %q_ref.1, s32[8,8]{1,0:T(8,128)} %bitcast.16, s32[4,4,4]{2,1,0:T(4,128)} %listed_ref.1), custom_call_target="tpu_custom_call" | custom-call | tf_op jit(solution)/shard_map/pallas_call | solution.py:521
  40.7 0.8 %copy_bitcast_fusion.1 = bf16[1,4,32,128]{3,2,1,0:T(8,128)(2,1)S(1)} fusion(bf16[4,32,128]{2,1,0:T(8,128)(2,1)} %shard_map.55), kind=kLoop, calls=%fused_computation.1 | loop fusion | bytes 65536
  41.5 0.6 %copy.10 = bf16[1,4,32,128]{3,1,2,0:T(4,128)(2,1)} copy(bf16[1,4,32,128]{3,2,1,0:T(8,128)(2,1)S(1)} %copy_bitcast_fusion.1) | data formatting | bytes 65536

commit v5 on v4

--- a/solution.py
+++ b/solution.py
@@ -150,7 +150,7 @@
 
 def fast_kernel(
     k_hbm, v_hbm, q_ref, ids_ref, listed_ref, out_ref,
-    kbuf, vbuf, kout, vout, kturn, qx, qall, bt, btx, bias, o_buf, o_rx,
+    kbuf, vbuf, kout, vout, qx, qall, bt, btx, bias, o_buf, o_rx,
     ts_buf, ts_rx, cs_buf, cs_rx, red_buf, tot_rx, wt, hot_ref,
     loc_sem, kv_send, kv_recv, in_send, in_recv,
     o_send, o_recv, ts_sem, cs_send, cs_recv, tot_send, tot_recv,
@@ -187,7 +187,7 @@
                         src.at[:, column], out.at[half, hh], loc_sem.at[1, number]))
                 else:
                     copies.append(pltpu.make_async_remote_copy(
-                        src_ref=out.at[half, hh], dst_ref=dst.at[half, hh, pl.ds(rows, rows)],
+                        src_ref=src.at[:, column], dst_ref=dst.at[half, hh, pl.ds(rows, rows)],
                         send_sem=kv_send.at[number], recv_sem=kv_recv.at[number],
                         device_id=(x, sib), device_id_type=MESH))
         return copies
@@ -200,7 +200,7 @@
     own_kv = [kv_copies(0, 0), kv_copies(1, 0)]
     out_kv = [kv_copies(0, 1), kv_copies(1, 1)]
     far_kv = [kv_copies(0, 2), kv_copies(1, 2)]
-    for copy in out_kv[0] + out_kv[1] + own_kv[0] + own_kv[1]:
+    for copy in own_kv[0] + own_kv[1] + out_kv[0] + out_kv[1]:
         copy.start()
 
     barrier = pltpu.get_barrier_semaphore()
@@ -240,21 +240,9 @@
                 live = live | (held == table)
             bt[side, turn] = jnp.where(live, 0.0, dead)
 
-    key_tile = lax.broadcasted_iota(jnp.int32, (128, 2 * rows), 1) // TILE
-    hot = key_tile == lax.broadcasted_iota(jnp.int32, (128, 2 * rows), 0)
+    key_tile = lax.broadcasted_iota(jnp.int32, (2 * rows, 128), 0) // TILE
+    hot = key_tile == lax.broadcasted_iota(jnp.int32, (2 * rows, 128), 1)
     hot_ref[...] = jnp.where(hot, 1.0, 0.0).astype(jnp.bfloat16)
-
-    def turn_keys(half, side):
-        def turn(n, carry):
-            hh, first = n // 2, pl.multiple_of(side * rows + lax.rem(n, 2) * (rows // 2), 128)
-            for head in range(2):
-                @pl.when(hh == head)
-                def _():
-                    part = kbuf[half, head, pl.ds(first, rows // 2), :]
-                    kturn[half, head, :, pl.ds(first, rows // 2)] = part.T
-            return carry
-
-        lax.fori_loop(0, 4, turn, 0)
 
     def regroup(rows_in):
         count_in = rows_in.shape[0]
@@ -277,8 +265,6 @@
 
     place_queries(0, q_ref, c * 2 * wide)
     pl.semaphore_wait(barrier, 2 * clus - 1)
-    for copy in out_kv[0] + out_kv[1]:
-        copy.wait()
 
     small = [
         remote(bt.at[0, 1], btx.at[0], in_send.at[0], in_recv.at[0], (x, sib)),
@@ -287,24 +273,25 @@
         remote(q_ref.at[:, pl.ds(pl.multiple_of(c * 2 * wide, 128), 2 * wide)], qx,
                in_send.at[3], in_recv.at[3], (1 - x, i)),
     ]
-    for copy in small + far_kv[0] + far_kv[1]:
+    for copy in small[:1] + small[3:] + far_kv[0] + small[1:3] + far_kv[1]:
         copy.start()
 
-    for copy in own_kv[0] + own_kv[1]:
-        copy.wait()
-
-    def add_up(n, carry):
-        half, hh = n // 2, lax.rem(n, 2)
-        for m, (buf, out) in enumerate(((kbuf, kout), (vbuf, vout))):
-            for part, core in ((buf[half, hh, :rows], c), (out[half, hh], 1 - c)):
-                ts_buf[half, m, 2 * core + hh] = jnp.sum(
-                    part.astype(jnp.float32).reshape(tiles, TILE, DH), axis=1)
-        return carry
-
-    lax.fori_loop(0, 4, add_up, 0)
-    turn_keys(0, 0)
     ts_copy = remote(ts_buf.at[1], ts_rx, ts_sem.at[0], ts_sem.at[1], (1 - x, i))
-    ts_copy.start()
+
+    def tile_sums():
+        for copy in own_kv[1] + out_kv[0] + out_kv[1]:
+            copy.wait()
+
+        def add_up(n, carry):
+            half, hh = n // 2, lax.rem(n, 2)
+            for m, (buf, out) in enumerate(((kbuf, kout), (vbuf, vout))):
+                for part, core in ((buf[half, hh, :rows], c), (out[half, hh], 1 - c)):
+                    ts_buf[half, m, 2 * core + hh] = jnp.sum(
+                        part.astype(jnp.float32).reshape(tiles, TILE, DH), axis=1)
+            return carry
+
+        lax.fori_loop(0, 4, add_up, 0)
+        ts_copy.start()
 
     square = lax.broadcasted_iota(jnp.int32, (128, 128), 0) == lax.broadcasted_iota(
         jnp.int32, (128, 128), 1)
@@ -322,8 +309,8 @@
         ]
         masks = jnp.concatenate(masks, axis=0).astype(jnp.bfloat16)
         queries = jnp.concatenate([qall[half, hh, pl.ds(start, span), :], masks], axis=1)
-        keys = jnp.concatenate([kturn[half, hh], hot_ref[...]], axis=0)
-        scores = jnp.dot(queries, keys, preferred_element_type=jnp.float32)
+        keys = jnp.concatenate([kbuf[half, hh], hot_ref[...]], axis=1)
+        scores = lax.dot_general(queries, keys, nt, preferred_element_type=jnp.float32)
         top = jnp.maximum(jnp.max(scores, axis=1, keepdims=True), lowest_top) * log2_scale
         top = top.astype(jnp.bfloat16).astype(jnp.float32)
         weights = jnp.exp2(scores * log2_scale - top).astype(jnp.bfloat16)
@@ -341,7 +328,7 @@
             after.append(held)
             for j in range(4):
                 first = 128 * n + 32 * j
-                place = pl.ds(pl.multiple_of(hh * 32, 32), 32)
+                place = pl.ds(hh * 32, 32)
                 o_buf[half * clus + pair * 8 + n * 4 + j, place, :] = numer[
                     first : first + 32, :DH].astype(jnp.bfloat16)
         return tuple(after)
@@ -359,10 +346,11 @@
             pltpu.make_async_copy(src, o_rx.at[c, slot], o_recv).start()
 
     def first_half():
+        for copy in own_kv[0]:
+            copy.wait()
         small[0].wait_recv()
         for copy in far_kv[0]:
             copy.wait_recv()
-        turn_keys(0, 1)
         bias[0] = bt[0, 0] + btx[0]
 
     def second_half():
@@ -371,8 +359,6 @@
         for copy in far_kv[1]:
             copy.wait_recv()
         place_queries(1, qx, 0)
-        turn_keys(1, 0)
-        turn_keys(1, 1)
         bias[1] = btx[1] + btx[2]
 
     line = lax.broadcasted_iota(jnp.int32, (128, 128), 0)
@@ -426,7 +412,7 @@
         tot_rx[i] = reduced
         lax.fori_loop(1, clus, start_tot, 0)
 
-    hooks = ((first_half,), (cluster_sums,), (reduce_sums, second_half))
+    hooks = ((first_half,), (tile_sums,), (second_half, cluster_sums), (reduce_sums,))
 
     def step(n, carry):
         half, pair = n // 2, lax.rem(n + far, 2)
@@ -437,8 +423,9 @@
                     work()
 
         blank = jnp.zeros((16, 128), jnp.float32)
-        stats = lax.fori_loop(
-            0, 2, lambda hh, held: attend(half, pair, hh, held), (blank, blank))
+        stats = (blank, blank)
+        for hh in range(2):
+            stats = attend(half, pair, hh, stats)
         for n in range(2):
             packed = stats[n].astype(jnp.bfloat16)
             for j in range(4):
@@ -528,7 +515,6 @@
             pltpu.VMEM((2, 2, 2 * rows, DH), bf16),
             pltpu.VMEM((2, 2, rows, DH), bf16),
             pltpu.VMEM((2, 2, rows, DH), bf16),
-            pltpu.VMEM((2, 2, DH, 2 * rows), bf16),
             pltpu.VMEM((query_count, 2 * GROUP * DH), bf16),
             pltpu.VMEM((2, 2, query_count * GROUP, DH), bf16),
             pltpu.VMEM((2, 2, 2 * blocks, 128), f32),
@@ -543,7 +529,7 @@
             pltpu.VMEM((8, DH), f32),
             pltpu.VMEM((clus, 8, DH), f32),
             pltpu.VMEM((8, 128, 128), f32),
-            pltpu.VMEM((128, 2 * rows), bf16),
+            pltpu.VMEM((2 * rows, 128), bf16),
             dma((2, 8)), dma((8,)), dma((8,)), dma((4,)), dma((4,)),
             dma, dma, dma((2,)), dma, dma, dma, dma,
         ],

time: 42.3 us -> 37.5 us (0.89)
  Pallas kernels: 40.7 us -> 35.9 us
    pallas_call x1, Pallas kernels: 40.7 us -> 35.9 us  [fast_local(): pl.pallas_call(fast_kernel, out_shape=jax.ShapeDtypeStruct((heads, share,...]
where the time goes in v5:
time: 37.5 us; the launch traced here: 37.3 us
  Pallas kernels  35.9 us (96%)
  local copies, waits for them, and re-layouts  1.4 us (4%)
    pallas_call x1, Pallas kernels, fast_local(): pl.pallas_call(fast_kernel, out_shape=jax.ShapeDtypeStruct((heads, share,...  35.9 us
    unnamed x2, local copies, waits for them, and re-layouts  1.4 us

profile of v5, /device:TPU:0, one launch (start us, length us, event | category | flops | bytes accessed | tf_op | source)
XLA Modules:
  0.0 37.3 jit_solution(16325842095829677778)
XLA Ops:
  0.0 35.9 %shard_map.55 = bf16[4,32,128]{2,1,0:T(8,128)(2,1)} custom-call(bf16[1024,1024]{1,0:T(8,128)(2,1)} %bitcast.14, bf16[1024,1024]{1,0:T(8,128)(2,1)} %bitcast.15, bf16[64,4096]{1,0:T(8,128)(2,1)} %q_ref.1, s32[8,8]{1,0:T(8,128)} %bitcast.16, s32[4,4,4]{2,1,0:T(4,128)} %listed_ref.1), custom_call_target="tpu_custom_call" | custom-call | tf_op jit(solution)/shard_map/pallas_call | solution.py:508
  35.9 0.8 %copy_bitcast_fusion.1 = bf16[1,4,32,128]{3,2,1,0:T(8,128)(2,1)S(1)} fusion(bf16[4,32,128]{2,1,0:T(8,128)(2,1)} %shard_map.55), kind=kLoop, calls=%fused_computation.1 | loop fusion | bytes 65536
  36.7 0.6 %copy.10 = bf16[1,4,32,128]{3,1,2,0:T(4,128)(2,1)} copy(bf16[1,4,32,128]{3,2,1,0:T(8,128)(2,1)S(1)} %copy_bitcast_fusion.1) | data formatting | bytes 65536

commit v6 on v5

--- a/solution.py
+++ b/solution.py
@@ -150,7 +150,7 @@
 
 def fast_kernel(
     k_hbm, v_hbm, q_ref, ids_ref, listed_ref, out_ref,
-    kbuf, vbuf, kout, vout, qx, qall, bt, btx, bias, o_buf, o_rx,
+    kbuf, vbuf, kout, vout, qall, bt, btx, bias, o_buf, o_rx,
     ts_buf, ts_rx, cs_buf, cs_rx, red_buf, tot_rx, wt, hot_ref,
     loc_sem, kv_send, kv_recv, in_send, in_recv,
     o_send, o_recv, ts_sem, cs_send, cs_recv, tot_send, tot_recv,
@@ -249,29 +249,28 @@
         split = rows_in.astype(jnp.float32).reshape(count_in, GROUP, DH)
         return split.reshape(count_in * GROUP, DH).astype(jnp.bfloat16)
 
-    def place_queries(half, source, first):
+    def place_queries(first):
         def block_of(n, carry):
             hh, block = n // 4, lax.rem(n, 4)
             for head in range(2):
                 @pl.when(hh == head)
                 def _():
                     columns = pl.ds(pl.multiple_of(first + head * wide, 128), wide)
-                    taken = source[pl.ds(pl.multiple_of(block * QBLK, QBLK), QBLK), columns]
-                    qall[half, head, pl.ds(pl.multiple_of(block * 128, 128), 128), :] = regroup(
+                    taken = q_ref[pl.ds(pl.multiple_of(block * QBLK, QBLK), QBLK), columns]
+                    qall[0, head, pl.ds(pl.multiple_of(block * 128, 128), 128), :] = regroup(
                         taken)
             return carry
 
         lax.fori_loop(0, 8, block_of, 0)
 
-    place_queries(0, q_ref, c * 2 * wide)
+    place_queries(c * 2 * wide)
     pl.semaphore_wait(barrier, 2 * clus - 1)
 
     small = [
         remote(bt.at[0, 1], btx.at[0], in_send.at[0], in_recv.at[0], (x, sib)),
         remote(bt.at[1, 0], btx.at[1], in_send.at[1], in_recv.at[1], (1 - x, i)),
         remote(bt.at[1, 1], btx.at[2], in_send.at[2], in_recv.at[2], (1 - x, sib)),
-        remote(q_ref.at[:, pl.ds(pl.multiple_of(c * 2 * wide, 128), 2 * wide)], qx,
-               in_send.at[3], in_recv.at[3], (1 - x, i)),
+        remote(qall.at[0], qall.at[1], in_send.at[3], in_recv.at[3], (1 - x, i)),
     ]
     for copy in small[:1] + small[3:] + far_kv[0] + small[1:3] + far_kv[1]:
         copy.start()
@@ -279,7 +278,7 @@
     ts_copy = remote(ts_buf.at[1], ts_rx, ts_sem.at[0], ts_sem.at[1], (1 - x, i))
 
     def tile_sums():
-        for copy in own_kv[1] + out_kv[0] + out_kv[1]:
+        for copy in own_kv[0] + own_kv[1] + out_kv[0] + out_kv[1]:
             copy.wait()
 
         def add_up(n, carry):
@@ -346,8 +345,6 @@
             pltpu.make_async_copy(src, o_rx.at[c, slot], o_recv).start()
 
     def first_half():
-        for copy in own_kv[0]:
-            copy.wait()
         small[0].wait_recv()
         for copy in far_kv[0]:
             copy.wait_recv()
@@ -358,7 +355,6 @@
             copy.wait_recv()
         for copy in far_kv[1]:
             copy.wait_recv()
-        place_queries(1, qx, 0)
         bias[1] = btx[1] + btx[2]
 
     line = lax.broadcasted_iota(jnp.int32, (128, 128), 0)
@@ -412,24 +408,26 @@
         tot_rx[i] = reduced
         lax.fori_loop(1, clus, start_tot, 0)
 
-    hooks = ((first_half,), (tile_sums,), (second_half, cluster_sums), (reduce_sums,))
+    hooks = ((0, first_half), (2, second_half))
+    late_hooks = ((0, cluster_sums), (1, reduce_sums))
+    tile_sums()
 
     def step(n, carry):
         half, pair = n // 2, lax.rem(n + far, 2)
-        for number, hook in enumerate(hooks):
-            @pl.when(n == number)
-            def _():
-                for work in hook:
-                    work()
+        for number, work in hooks:
+            pl.when(n == number)(work)
 
         blank = jnp.zeros((16, 128), jnp.float32)
         stats = (blank, blank)
         for hh in range(2):
             stats = attend(half, pair, hh, stats)
-        for n in range(2):
-            packed = stats[n].astype(jnp.bfloat16)
+        for m in range(2):
+            packed = stats[m].astype(jnp.bfloat16)
             for j in range(4):
-                o_buf[half * clus + pair * 8 + n * 4 + j, 64:80, :] = packed
+                o_buf[half * clus + pair * 8 + m * 4 + j, 64:80, :] = packed
+
+        for number, work in late_hooks:
+            pl.when(n == number)(work)
 
         def one_dest(k, inner):
             ship(half, pair * 8 + lax.rem(k + i, 8))
@@ -515,7 +513,6 @@
             pltpu.VMEM((2, 2, 2 * rows, DH), bf16),
             pltpu.VMEM((2, 2, rows, DH), bf16),
             pltpu.VMEM((2, 2, rows, DH), bf16),
-            pltpu.VMEM((query_count, 2 * GROUP * DH), bf16),
             pltpu.VMEM((2, 2, query_count * GROUP, DH), bf16),
             pltpu.VMEM((2, 2, 2 * blocks, 128), f32),
             pltpu.VMEM((3, 2 * blocks, 128), f32),

time: 37.5 us -> 40.3 us (1.075)
  Pallas kernels: 35.9 us -> 38.7 us
    pallas_call x1, Pallas kernels: 35.9 us -> 38.7 us  [fast_local(): pl.pallas_call(fast_kernel, out_shape=jax.ShapeDtypeStruct((heads, share,...]
where the time goes in v6:
time: 40.3 us; the launch traced here: 40.1 us
  Pallas kernels  38.7 us (96%)
  local copies, waits for them, and re-layouts  1.4 us (3%)
    pallas_call x1, Pallas kernels, fast_local(): pl.pallas_call(fast_kernel, out_shape=jax.ShapeDtypeStruct((heads, share,...  38.7 us
    unnamed x2, local copies, waits for them, and re-layouts  1.4 us

profile of v6, /device:TPU:0, one launch (start us, length us, event | category | flops | bytes accessed | tf_op | source)
XLA Modules:
  0.0 40.1 jit_solution(17361121570258581408)
XLA Ops:
  0.0 38.7 %shard_map.55 = bf16[4,32,128]{2,1,0:T(8,128)(2,1)} custom-call(bf16[1024,1024]{1,0:T(8,128)(2,1)} %bitcast.14, bf16[1024,1024]{1,0:T(8,128)(2,1)} %bitcast.15, bf16[64,4096]{1,0:T(8,128)(2,1)} %q_ref.1, s32[8,8]{1,0:T(8,128)} %bitcast.16, s32[4,4,4]{2,1,0:T(4,128)} %listed_ref.1), custom_call_target="tpu_custom_call" | custom-call | tf_op jit(solution)/shard_map/pallas_call | solution.py:506
  38.7 0.8 %copy_bitcast_fusion.1 = bf16[1,4,32,128]{3,2,1,0:T(8,128)(2,1)S(1)} fusion(bf16[4,32,128]{2,1,0:T(8,128)(2,1)} %shard_map.55), kind=kLoop, calls=%fused_computation.1 | loop fusion | bytes 65536
  39.5 0.6 %copy.10 = bf16[1,4,32,128]{3,1,2,0:T(4,128)(2,1)} copy(bf16[1,4,32,128]{3,2,1,0:T(8,128)(2,1)S(1)} %copy_bitcast_fusion.1) | data formatting | bytes 65536

commit v7 on v6

--- a/solution.py
+++ b/solution.py
@@ -240,6 +240,16 @@
                 live = live | (held == table)
             bt[side, turn] = jnp.where(live, 0.0, dead)
 
+    pl.semaphore_wait(barrier, 2 * clus - 1)
+    small = [
+        remote(bt.at[0, 1], btx.at[0], in_send.at[0], in_recv.at[0], (x, sib)),
+        remote(bt.at[1, 0], btx.at[1], in_send.at[1], in_recv.at[1], (1 - x, i)),
+        remote(bt.at[1, 1], btx.at[2], in_send.at[2], in_recv.at[2], (1 - x, sib)),
+        remote(qall.at[0], qall.at[1], in_send.at[3], in_recv.at[3], (1 - x, i)),
+    ]
+    for copy in far_kv[0] + small[:3] + far_kv[1]:
+        copy.start()
+
     key_tile = lax.broadcasted_iota(jnp.int32, (2 * rows, 128), 0) // TILE
     hot = key_tile == lax.broadcasted_iota(jnp.int32, (2 * rows, 128), 1)
     hot_ref[...] = jnp.where(hot, 1.0, 0.0).astype(jnp.bfloat16)
@@ -264,21 +274,13 @@
         lax.fori_loop(0, 8, block_of, 0)
 
     place_queries(c * 2 * wide)
-    pl.semaphore_wait(barrier, 2 * clus - 1)
-
-    small = [
-        remote(bt.at[0, 1], btx.at[0], in_send.at[0], in_recv.at[0], (x, sib)),
-        remote(bt.at[1, 0], btx.at[1], in_send.at[1], in_recv.at[1], (1 - x, i)),
-        remote(bt.at[1, 1], btx.at[2], in_send.at[2], in_recv.at[2], (1 - x, sib)),
-        remote(qall.at[0], qall.at[1], in_send.at[3], in_recv.at[3], (1 - x, i)),
-    ]
-    for copy in small[:1] + small[3:] + far_kv[0] + small[1:3] + far_kv[1]:
-        copy.start()
+
+    small[3].start()
 
     ts_copy = remote(ts_buf.at[1], ts_rx, ts_sem.at[0], ts_sem.at[1], (1 - x, i))
 
     def tile_sums():
-        for copy in own_kv[0] + own_kv[1] + out_kv[0] + out_kv[1]:
+        for copy in own_kv[1] + out_kv[0] + out_kv[1]:
             copy.wait()
 
         def add_up(n, carry):
@@ -345,6 +347,8 @@
             pltpu.make_async_copy(src, o_rx.at[c, slot], o_recv).start()
 
     def first_half():
+        for copy in own_kv[0]:
+            copy.wait()
         small[0].wait_recv()
         for copy in far_kv[0]:
             copy.wait_recv()
@@ -408,9 +412,8 @@
         tot_rx[i] = reduced
         lax.fori_loop(1, clus, start_tot, 0)
 
-    hooks = ((0, first_half), (2, second_half))
-    late_hooks = ((0, cluster_sums), (1, reduce_sums))
-    tile_sums()
+    hooks = (
+        (0, first_half), (1, tile_sums), (2, second_half), (2, cluster_sums), (3, reduce_sums))
 
     def step(n, carry):
         half, pair = n // 2, lax.rem(n + far, 2)
@@ -425,9 +428,6 @@
             packed = stats[m].astype(jnp.bfloat16)
             for j in range(4):
                 o_buf[half * clus + pair * 8 + m * 4 + j, 64:80, :] = packed
-
-        for number, work in late_hooks:
-            pl.when(n == number)(work)
 
         def one_dest(k, inner):
             ship(half, pair * 8 + lax.rem(k + i, 8))

time: 40.3 us -> 37.5 us (0.931)
  Pallas kernels: 38.7 us -> 35.9 us
    pallas_call x1, Pallas kernels: 38.7 us -> 35.9 us  [fast_local(): pl.pallas_call(fast_kernel, out_shape=jax.ShapeDtypeStruct((heads, share,...]
where the time goes in v7:
time: 37.5 us; the launch traced here: 37.3 us
  Pallas kernels  35.9 us (96%)
  local copies, waits for them, and re-layouts  1.4 us (4%)
    pallas_call x1, Pallas kernels, fast_local(): pl.pallas_call(fast_kernel, out_shape=jax.ShapeDtypeStruct((heads, share,...  35.9 us
    unnamed x2, local copies, waits for them, and re-layouts  1.4 us

profile of v7, /device:TPU:0, one launch (start us, length us, event | category | flops | bytes accessed | tf_op | source)
XLA Modules:
  0.0 37.3 jit_solution(3820447620296571588)
XLA Ops:
  0.0 35.9 %shard_map.55 = bf16[4,32,128]{2,1,0:T(8,128)(2,1)} custom-call(bf16[1024,1024]{1,0:T(8,128)(2,1)} %bitcast.14, bf16[1024,1024]{1,0:T(8,128)(2,1)} %bitcast.15, bf16[64,4096]{1,0:T(8,128)(2,1)} %q_ref.1, s32[8,8]{1,0:T(8,128)} %bitcast.16, s32[4,4,4]{2,1,0:T(4,128)} %listed_ref.1), custom_call_target="tpu_custom_call" | custom-call | tf_op jit(solution)/shard_map/pallas_call | solution.py:506
  35.9 0.8 %copy_bitcast_fusion.1 = bf16[1,4,32,128]{3,2,1,0:T(8,128)(2,1)S(1)} fusion(bf16[4,32,128]{2,1,0:T(8,128)(2,1)} %shard_map.55), kind=kLoop, calls=%fused_computation.1 | loop fusion | bytes 65536
  36.7 0.6 %copy.10 = bf16[1,4,32,128]{3,1,2,0:T(4,128)(2,1)} copy(bf16[1,4,32,128]{3,2,1,0:T(8,128)(2,1)S(1)} %copy_bitcast_fusion.1) | data formatting | bytes 65536

commit v8 on v7

--- a/solution.py
+++ b/solution.py
@@ -413,7 +413,7 @@
         lax.fori_loop(1, clus, start_tot, 0)
 
     hooks = (
-        (0, first_half), (1, tile_sums), (2, second_half), (2, cluster_sums), (3, reduce_sums))
+        (0, first_half), (1, tile_sums), (2, second_half), (2, cluster_sums))
 
     def step(n, carry):
         half, pair = n // 2, lax.rem(n + far, 2)
@@ -437,6 +437,7 @@
         return carry
 
     lax.fori_loop(0, 4, step, 0)
+    reduce_sums()
     take_all(tot_rx, clus - 1, tot_recv)
     block, part = i // 4, lax.rem(i, 4)
     share = pl.ds(pl.multiple_of(part * 32, 32), 32)

time: 37.5 us -> 37.2 us (level)
  no operation moved by 1% of the time
where the time goes in v8:
time: 37.2 us; the launch traced here: 37 us
  Pallas kernels  35.6 us (96%)
  local copies, waits for them, and re-layouts  1.4 us (4%)
    pallas_call x1, Pallas kernels, fast_local(): pl.pallas_call(fast_kernel, out_shape=jax.ShapeDtypeStruct((heads, share,...  35.6 us
    unnamed x2, local copies, waits for them, and re-layouts  1.4 us

profile of v8, /device:TPU:0, one launch (start us, length us, event | category | flops | bytes accessed | tf_op | source)
XLA Modules:
  0.0 37.0 jit_solution(14804135705004773131)
XLA Ops:
  0.0 35.6 %shard_map.55 = bf16[4,32,128]{2,1,0:T(8,128)(2,1)} custom-call(bf16[1024,1024]{1,0:T(8,128)(2,1)} %bitcast.14, bf16[1024,1024]{1,0:T(8,128)(2,1)} %bitcast.15, bf16[64,4096]{1,0:T(8,128)(2,1)} %q_ref.1, s32[8,8]{1,0:T(8,128)} %bitcast.16, s32[4,4,4]{2,1,0:T(4,128)} %listed_ref.1), custom_call_target="tpu_custom_call" | custom-call | tf_op jit(solution)/shard_map/pallas_call | solution.py:507
  35.6 0.8 %copy_bitcast_fusion.1 = bf16[1,4,32,128]{3,2,1,0:T(8,128)(2,1)S(1)} fusion(bf16[4,32,128]{2,1,0:T(8,128)(2,1)} %shard_map.55), kind=kLoop, calls=%fused_computation.1 | loop fusion | bytes 65536
  36.3 0.6 %copy.10 = bf16[1,4,32,128]{3,1,2,0:T(4,128)(2,1)} copy(bf16[1,4,32,128]{3,2,1,0:T(8,128)(2,1)S(1)} %copy_bitcast_fusion.1) | data formatting | bytes 65536
